TPU v7x, 32 devices: a whole 2x2x4 slice. The times are simulated.
32 devices in a mesh: dp: 16 (over z, x, core), seq: 2 (over y).
Axes of the slice: x: 2, y: 2, z: 4, core: 2. Of those that a mesh axis runs over, the one named last changes fastest.
Arguments:
- tokens: bfloat16 [2, 16, 1024, 1024], P(None, 'dp', 'seq'), may hold values from -6 to 6
- lengths: int32 [2, 16], P(None, 'dp'), may hold values from 256 to 1024, as said below
- w_query: bfloat16 [1024, 1024], P(('dp', 'seq')), may hold values from -0.1875 to 0.1875
- w_key: bfloat16 [1024, 1024], P(('dp', 'seq')), may hold values from -0.1875 to 0.1875
- w_value: bfloat16 [1024, 1024], P(('dp', 'seq')), may hold values from -0.1875 to 0.1875
- w_out: bfloat16 [1024, 1024], P(('dp', 'seq')), may hold values from -3 to 3
- w_up: bfloat16 [1024, 4096], P(('dp', 'seq')), may hold values from -0.1875 to 0.1875
- w_down: bfloat16 [4096, 1024], P(('dp', 'seq')), may hold values from -0.09375 to 0.09375
- vectors: bfloat16 [8, 1024], P(None, ('dp', 'seq')), as said below
- up_bias: bfloat16 [4096], P(('dp', 'seq')), may hold values from -3 to 3
- cotangent: bfloat16 [2, 16, 1024, 1024], P(None, 'dp', 'seq'), may hold values from -6 to 6
Outputs:
- activations: bfloat16 [2, 16, 1024, 1024], P(None, 'dp', 'seq')
- grad_tokens: float32 [2, 16, 1024, 1024], P(None, 'dp', 'seq')
- grad_w_query: float32 [1024, 1024], P(('dp', 'seq'))
- grad_w_key: float32 [1024, 1024], P(('dp', 'seq'))
- grad_w_value: float32 [1024, 1024], P(('dp', 'seq'))
- grad_w_out: float32 [1024, 1024], P(('dp', 'seq'))
- grad_w_up: float32 [1024, 4096], P(('dp', 'seq'))
- grad_w_down: float32 [4096, 1024], P(('dp', 'seq'))
- grad_vectors: float32 [8, 1024], P(None, ('dp', 'seq'))
- grad_up_bias: float32 [4096], P(('dp', 'seq'))
Inputs may be any that keep to these rules, and one draw needn't show every extreme that they name: `lengths`: in every sequence column one of the 2 micro-batches, which one drawn from the seed, has length 1024; the others are drawn evenly. `vectors`: rows 3 and 6 lie near 1, the others near 0.
All inputs are finite; a program needn't handle non-finite values.
Results may differ from a plain program's by a relative error of at most 0.014.
Values may be sent and summed in bfloat16 or wider, within the bound.
A program may use at most 320 MiB of HBM per device.

v0:
```python
import math

import jax
import jax.numpy as jnp
from jax import lax
from jax.sharding import PartitionSpec as P

H = 16


EPSILON = 1e-05


def fetch_forward(w_query, w_key, w_value, w_out, w_up, w_down, vectors, up_bias):
    return (
        lax.all_gather(w_query, ("dp", "seq"), axis=0, tiled=True),
        lax.all_gather(w_key, ("dp", "seq"), axis=0, tiled=True),
        lax.all_gather(w_value, ("dp", "seq"), axis=0, tiled=True),
        lax.all_gather(w_out, ("dp", "seq"), axis=0, tiled=True),
        lax.all_gather(w_up, ("dp", "seq"), axis=0, tiled=True),
        lax.all_gather(w_down, ("dp", "seq"), axis=0, tiled=True),
        lax.all_gather(vectors, ("dp", "seq"), axis=1, tiled=True),
        lax.all_gather(up_bias, ("dp", "seq"), axis=0, tiled=True),
    )


def fetch_backward(w_query, w_key, w_value, w_out, w_up, w_down, vectors, up_bias):
    return (
        lax.all_gather(w_query, ("dp", "seq"), axis=0, tiled=True),
        lax.all_gather(w_key, ("dp", "seq"), axis=0, tiled=True),
        lax.all_gather(w_value, ("dp", "seq"), axis=0, tiled=True),
        lax.all_gather(w_out, ("dp", "seq"), axis=0, tiled=True),
        lax.all_gather(w_up, ("dp", "seq"), axis=0, tiled=True),
        lax.all_gather(w_down, ("dp", "seq"), axis=0, tiled=True),
        lax.all_gather(vectors, ("dp", "seq"), axis=1, tiled=True),
        lax.all_gather(up_bias, ("dp", "seq"), axis=0, tiled=True),
    )


def norm_forward(inputs, gain, shift):
    center = inputs - jnp.mean(inputs, axis=-1, keepdims=True)
    inverse = lax.rsqrt(jnp.mean(center * center, axis=-1, keepdims=True) + EPSILON)
    normed = center * inverse
    return (normed * gain + shift, normed, inverse)


def norm_backward(grad_out, normed, inverse, gain):
    grad_norm = grad_out * gain
    inner = (
        grad_norm
        - jnp.mean(grad_norm, axis=-1, keepdims=True)
        - normed * jnp.mean(grad_norm * normed, axis=-1, keepdims=True)
    )
    return (inner * inverse, jnp.sum(grad_out * normed, axis=0), jnp.sum(grad_out, axis=0))


def score_heads(query_heads, key_heads, key_valid, factor):
    scores = (
        jnp.einsum("qhd,khd->hqk", query_heads, key_heads, preferred_element_type=jnp.float32)
        * factor
    )
    return jnp.where(key_valid[None, None, :], scores, -1000000000.0)


def per_device(
    tokens, lengths, w_query, w_key, w_value, w_out, w_up, w_down, vectors, up_bias, cotangent
):
    micro = tokens.shape[0]
    slot = tokens.shape[2]
    width = tokens.shape[3]
    hidden_units = w_up.shape[1]
    heads = H
    head_dim = width // heads
    factor = 1.0 / math.sqrt(head_dim)
    positions = lax.axis_index("seq") * slot + jnp.arange(slot, dtype=jnp.int32)
    f32 = jnp.float32
    sums = [
        jnp.zeros((width, width), f32),
        jnp.zeros((width, width), f32),
        jnp.zeros((width, width), f32),
        jnp.zeros((width, width), f32),
        jnp.zeros((width, hidden_units), f32),
        jnp.zeros((hidden_units, width), f32),
        jnp.zeros((8, width), f32),
        jnp.zeros((hidden_units,), f32),
    ]
    outputs = []
    grad_list = []
    for micro_index in range(micro):
        full_query, full_key, full_value, full_out, full_up, full_down, full_vectors, full_bias = (
            fetch_forward(w_query, w_key, w_value, w_out, w_up, w_down, vectors, up_bias)
        )
        vec_f = full_vectors.astype(f32)
        bias_f = full_bias.astype(f32)
        rows_in = tokens[micro_index, 0]
        length = lengths[micro_index, 0]
        valid = (positions < length)[:, None].astype(f32)
        query = (jnp.dot(rows_in, full_query, preferred_element_type=f32) + vec_f[0]).astype(
            jnp.bfloat16
        )
        keys_own = jnp.dot(rows_in, full_key, preferred_element_type=f32).astype(jnp.bfloat16)
        vals_own = (jnp.dot(rows_in, full_value, preferred_element_type=f32) + vec_f[1]).astype(
            jnp.bfloat16
        )
        keys_all, vals_all = (
            lax.all_gather(keys_own, "seq", axis=0, tiled=True),
            lax.all_gather(vals_own, "seq", axis=0, tiled=True),
        )
        total_len = keys_all.shape[0]
        key_valid = jnp.arange(total_len, dtype=jnp.int32) < length
        query_heads = query.reshape(slot, heads, head_dim)
        key_heads = keys_all.reshape(total_len, heads, head_dim)
        val_heads = vals_all.reshape(total_len, heads, head_dim)
        scores = score_heads(query_heads, key_heads, key_valid, factor)
        top = jnp.max(scores, axis=-1, keepdims=True)
        log_total = top + jnp.log(jnp.sum(jnp.exp(scores - top), axis=-1, keepdims=True))
        probs = jnp.exp(scores - log_total).astype(jnp.bfloat16)
        context = (
            jnp.einsum("hqk,khd->qhd", probs, val_heads, preferred_element_type=f32)
            .reshape(slot, width)
            .astype(jnp.bfloat16)
        )
        attention = jnp.dot(context, full_out, preferred_element_type=f32) + vec_f[2]
        hidden, normed_one, inverse_one = norm_forward(
            rows_in.astype(f32) + attention, vec_f[3], vec_f[4]
        )
        hidden_low = hidden.astype(jnp.bfloat16)
        upper = jnp.dot(hidden_low, full_up, preferred_element_type=f32) + bias_f
        active = jax.nn.gelu(upper).astype(jnp.bfloat16)
        lowered = jnp.dot(active, full_down, preferred_element_type=f32) + vec_f[5]
        result, normed_two, inverse_two = norm_forward(hidden + lowered, vec_f[6], vec_f[7])
        outputs.append((result * valid).astype(jnp.bfloat16))
        full_query, full_key, full_value, full_out, full_up, full_down, full_vectors, full_bias = (
            fetch_backward(w_query, w_key, w_value, w_out, w_up, w_down, vectors, up_bias)
        )
        vec_f = full_vectors.astype(f32)
        grad_out = cotangent[micro_index, 0].astype(f32) * valid
        grad_res2, grad_gain2, grad_shift2 = norm_backward(
            grad_out, normed_two, inverse_two, vec_f[6]
        )
        grad_down = grad_res2.astype(jnp.bfloat16)
        grad_bias2 = jnp.sum(grad_down.astype(f32), axis=0)
        sums[5] = sums[5] + jnp.einsum("sf,sd->fd", active, grad_down, preferred_element_type=f32)
        grad_active = jnp.einsum("sd,fd->sf", grad_down, full_down, preferred_element_type=f32)
        gelu_pull = jax.vjp(jax.nn.gelu, upper)[1]
        grad_upper = gelu_pull(grad_active)[0].astype(jnp.bfloat16)
        sums[7] = sums[7] + jnp.sum(grad_upper.astype(f32), axis=0)
        sums[4] = sums[4] + jnp.einsum(
            "sd,sf->df", hidden_low, grad_upper, preferred_element_type=f32
        )
        grad_hidden = grad_res2 + jnp.einsum(
            "sf,df->sd", grad_upper, full_up, preferred_element_type=f32
        )
        grad_res1, grad_gain1, grad_shift1 = norm_backward(
            grad_hidden, normed_one, inverse_one, vec_f[3]
        )
        grad_att = grad_res1.astype(jnp.bfloat16)
        grad_bias_out = jnp.sum(grad_att.astype(f32), axis=0)
        sums[3] = sums[3] + jnp.einsum("sd,se->de", context, grad_att, preferred_element_type=f32)
        grad_context = jnp.einsum(
            "se,de->sd", grad_att, full_out, preferred_element_type=f32
        ).astype(jnp.bfloat16)
        grad_ctx_heads = grad_context.reshape(slot, heads, head_dim)
        scores_again = score_heads(query_heads, key_heads, key_valid, factor)
        full_probs = jnp.exp(scores_again - log_total)
        probs_low = full_probs.astype(jnp.bfloat16)
        grad_probs = jnp.einsum(
            "qhd,khd->hqk", grad_ctx_heads, val_heads, preferred_element_type=f32
        )
        grad_val_term = jnp.einsum(
            "hqk,qhd->khd", probs_low, grad_ctx_heads, preferred_element_type=f32
        )
        row_inner = jnp.sum(full_probs * grad_probs, axis=-1, keepdims=True)
        grad_scores = (full_probs * (grad_probs - row_inner)).astype(jnp.bfloat16)
        grad_query = (
            (
                jnp.einsum("hqk,khd->qhd", grad_scores, key_heads, preferred_element_type=f32)
                * factor
            )
            .reshape(slot, width)
            .astype(jnp.bfloat16)
        )
        grad_key_term = (
            jnp.einsum("hqk,qhd->khd", grad_scores, query_heads, preferred_element_type=f32)
            * factor
        )
        grad_keys, grad_vals = (
            lax.psum_scatter(
                grad_key_term.reshape(total_len, width).astype(jnp.bfloat16),
                "seq",
                scatter_dimension=0,
                tiled=True,
            ).astype(jnp.float32),
            lax.psum_scatter(
                grad_val_term.reshape(total_len, width).astype(jnp.bfloat16),
                "seq",
                scatter_dimension=0,
                tiled=True,
            ).astype(jnp.float32),
        )
        grad_keys = grad_keys.astype(jnp.bfloat16)
        grad_vals = grad_vals.astype(jnp.bfloat16)
        grad_bias_query = jnp.sum(grad_query.astype(f32), axis=0)
        grad_bias_vals = jnp.sum(grad_vals.astype(f32), axis=0)
        sums[0] = sums[0] + jnp.einsum("sd,se->de", rows_in, grad_query, preferred_element_type=f32)
        sums[1] = sums[1] + jnp.einsum("sd,se->de", rows_in, grad_keys, preferred_element_type=f32)
        sums[2] = sums[2] + jnp.einsum("sd,se->de", rows_in, grad_vals, preferred_element_type=f32)
        sums[6] = sums[6] + jnp.stack(
            [
                grad_bias_query,
                grad_bias_vals,
                grad_bias_out,
                grad_gain1,
                grad_shift1,
                grad_bias2,
                grad_gain2,
                grad_shift2,
            ]
        )
        grad_rows = grad_res1 + jnp.einsum(
            "se,de->sd", grad_query, full_query, preferred_element_type=f32
        )
        grad_rows = grad_rows + jnp.einsum(
            "se,de->sd", grad_keys, full_key, preferred_element_type=f32
        )
        grad_rows = grad_rows + jnp.einsum(
            "se,de->sd", grad_vals, full_value, preferred_element_type=f32
        )
        grad_list.append(grad_rows)
    shares = (
        lax.psum_scatter(sums[0], ("dp", "seq"), scatter_dimension=0, tiled=True),
        lax.psum_scatter(sums[1], ("dp", "seq"), scatter_dimension=0, tiled=True),
        lax.psum_scatter(sums[2], ("dp", "seq"), scatter_dimension=0, tiled=True),
        lax.psum_scatter(sums[3], ("dp", "seq"), scatter_dimension=0, tiled=True),
        lax.psum_scatter(sums[4], ("dp", "seq"), scatter_dimension=0, tiled=True),
        lax.psum_scatter(sums[5], ("dp", "seq"), scatter_dimension=0, tiled=True),
        lax.psum_scatter(sums[6], ("dp", "seq"), scatter_dimension=1, tiled=True),
        lax.psum_scatter(sums[7], ("dp", "seq"), scatter_dimension=0, tiled=True),
    )
    activations = jnp.stack(outputs)[:, None]
    grad_tokens = jnp.stack(grad_list)[:, None]
    return (
        activations,
        grad_tokens,
        shares[0],
        shares[1],
        shares[2],
        shares[3],
        shares[4],
        shares[5],
        shares[6],
        shares[7],
    )


def solution(mesh):
    placed = (
        P(None, "dp", "seq", None),
        P(None, "dp"),
        P(("dp", "seq"), None),
        P(("dp", "seq"), None),
        P(("dp", "seq"), None),
        P(("dp", "seq"), None),
        P(("dp", "seq"), None),
        P(("dp", "seq"), None),
        P(None, ("dp", "seq")),
        P(("dp", "seq")),
        P(None, "dp", "seq", None),
    )
    return jax.shard_map(
        per_device,
        mesh=mesh,
        in_specs=placed,
        out_specs=(
            P(None, "dp", "seq", None),
            P(None, "dp", "seq", None),
            P(("dp", "seq"), None),
            P(("dp", "seq"), None),
            P(("dp", "seq"), None),
            P(("dp", "seq"), None),
            P(("dp", "seq"), None),
            P(("dp", "seq"), None),
            P(None, ("dp", "seq")),
            P(("dp", "seq")),
        ),
        check_vma=False,
    )
```

profile of v0, /device:TPU:5, one launch (start us, length us, event | category | flops | bytes accessed | tf_op | source)
XLA Modules:
  0.0 2258.9 jit_solution(10580955430075519356)
XLA Ops:
  9.4 61.5 %all-gather = bf16[32,32,8]{1,2,0:T(8,128)(2,1)S(1)} all-gather(bf16[1,32,8]{1,2,0:T(8,128)(2,1)} %bitcast.278), channel_id=1, replica_groups=mesh['dp'=16,'seq'=2] {'dp','seq'}, dimensions={0}, use_global_device_ids=true | all-gather | bytes 16896 | tf_op jit(solution)/shard_map/all_gather | solution.py:22
  71.6 4.3 add_convert_fusion.1
  76.0 3.8 add_convert_fusion.3
  79.9 47.9 %all-gather.19.cloned.1.call-done = bf16[1024,1024]{1,0:T(8,128)(2,1)} async-done(((bf16[32,1024]{1,0:T(8,128)(2,1)}), bf16[1024,1024]{1,0:T(8,128)(2,1)}) %all-gather.19.cloned.1.call-update) | async-done | bytes 2097168 | tf_op jit(solution)/shard_map/all_gather | solution.py:17
  127.8 3.9 convolution_convert_fusion.5
  131.8 3.9 convolution_convert_fusion.7
  138.4 60.2 %all-gather.1 = bf16[32,1,128]{2,1,0:T(2,128)(2,1)S(1)} all-gather(bf16[1,1,128]{2,1,0:T(2,128)(2,1)S(1)} %bitcast.279), channel_id=1, replica_groups=mesh['dp'=16,'seq'=2] {'dp','seq'}, dimensions={0}, use_global_device_ids=true | all-gather | bytes 8448 | tf_op jit(solution)/shard_map/all_gather | solution.py:23
  201.8 3.8 add_convert_fusion
  207.3 4.2 add_convert_fusion.2
  213.8 5.1 all-gather.29.cloned.1.call-done
  218.9 3.9 copy.60
  222.8 30.6 %all-gather.15.cloned.1.call-done = bf16[1024,1024]{1,0:T(8,128)(2,1)} async-done(((bf16[512,1024]{1,0:T(8,128)(2,1)}), bf16[1024,1024]{1,0:T(8,128)(2,1)}) %all-gather.15.cloned.1.call-update) | async-done | bytes 2097168 | tf_op jit(solution)/shard_map/all_gather | solution.py:107
  253.4 3.9 copy.57
  257.4 30.6 %all-gather.31.cloned.1.call-done = bf16[1024,1024]{1,0:T(8,128)(2,1)} async-done(((bf16[512,1024]{1,0:T(8,128)(2,1)}), bf16[1024,1024]{1,0:T(8,128)(2,1)}) %all-gather.31.cloned.1.call-update) | async-done | bytes 2097168 | tf_op jit(solution)/shard_map/all_gather | solution.py:106
  290.8 31.8 %all-gather.21.cloned.1.call-done = bf16[1024,1024]{1,0:T(8,128)(2,1)} async-done(((bf16[512,1024]{1,0:T(8,128)(2,1)}), bf16[1024,1024]{1,0:T(8,128)(2,1)}) %all-gather.21.cloned.1.call-update) | async-done | bytes 2097168 | tf_op jit(solution)/shard_map/all_gather | solution.py:106
  322.7 3.9 copy.59
  326.6 15.3 fusion
  341.9 14.6 exponential_reduce_fusion.1
  356.6 15.8 convolution_convert_fusion.6
  372.3 11.4 all-gather.23.cloned.1.call-done
  383.7 3.5 fusion.114
  389.0 13.6 fusion.1
  402.5 14.8 exponential_reduce_fusion
  417.4 14.2 convolution_convert_fusion.4
  431.5 3.7 fusion.112
  435.6 27.5 %all-gather.25.cloned.1.call-done = bf16[1024,4096]{1,0:T(8,128)(2,1)} async-done(((bf16[32,4096]{1,0:T(8,128)(2,1)}), bf16[1024,4096]{1,0:T(8,128)(2,1)}) %all-gather.25.cloned.1.call-update) | async-done | bytes 8388624 | tf_op jit(solution)/shard_map/all_gather | solution.py:20
  463.2 11.9 fusion.106
  475.0 67.1 %all-gather.27.cloned.1.call-done = bf16[4096,1024]{1,0:T(8,128)(2,1)} async-done(((bf16[128,1024]{1,0:T(8,128)(2,1)}), bf16[4096,1024]{1,0:T(8,128)(2,1)}) %all-gather.27.cloned.1.call-update) | async-done | bytes 8388624 | tf_op jit(solution)/shard_map/all_gather | solution.py:21
  542.2 11.5 fusion.115
  553.7 7.1 fusion.102
  560.8 8.6 fusion.113
  574.1 3.8 convert_reduce_fusion.2
  577.9 15.5 convert_reduce_fusion.1
  593.4 11.9 multiply_reduce_fusion.3
  605.3 16.3 convert_reduce_fusion
  621.7 13.3 convert_reduce_fusion.7
  646.8 15.3 convolution_convert_fusion.1
  662.2 16.0 convolution_convert_fusion
  678.2 23.4 %multiply_reduce_fusion.1 = (f32[16,512]{1,0:T(8,128)S(1)}, f32[16,512,1024]{2,1,0:T(8,128)}) fusion(f32[16,512,1024]{2,1,0:T(8,128)} %get-tuple-element.93, f32[16,512]{1,0:T(8,128)S(1)} %copy-done.40, pred[1024]{0:T(1024)(128)(4,1)S(1)} %copy-done.48, bf16[512,16,64]{0,2,1:T(8,128)(2,1)S(1)} %bitcast.220, bf16[1024,16,64]{0,2,1:T(8,128)(2,1)S(1)} %bitcast.212), kind=kOutput, calls=%fused_computation.3 | convolution fusion | flops 1115676672 | bytes 70321152 | tf_op jit(solution)/shard_map/qhd,khd->hqk/dot_general | solution.py:167
  701.7 28.9 %multiply_convert_fusion.1 = bf16[16,512,1024]{2,1,0:T(8,128)(2,1)} fusion(f32[16,512,1024]{2,1,0:T(8,128)} %get-tuple-element.103, f32[16,512,1024]{2,1,0:T(8,128)} %get-tuple-element.93, f32[16,512]{1,0:T(8,128)S(1)} %get-tuple-element.102, f32[16,512]{1,0:T(8,128)S(1)} %copy-done.40, pred[1024]{0:T(1024)(128)(4,1)S(1)} %copy-done.48), kind=kLoop, calls=%fused_computation.2 | loop fusion | flops 50331648 | bytes 83952640 | tf_op jit(solution)/shard_map/convert_element_type | solution.py:174
  730.5 10.3 multiply_convert_fusion.5
  740.8 23.2 %multiply_reduce_fusion = (f32[16,512]{1,0:T(8,128)S(1)}, f32[16,512,1024]{2,1,0:T(8,128)}) fusion(f32[16,512,1024]{2,1,0:T(8,128)} %get-tuple-element.87, f32[16,512]{1,0:T(8,128)S(1)} %log_add_fusion, pred[1024]{0:T(1024)(128)(4,1)S(1)} %iota_compare_fusion, bf16[512,16,64]{0,2,1:T(8,128)(2,1)S(1)} %bitcast.218, bf16[1024,16,64]{0,2,1:T(8,128)(2,1)S(1)} %bitcast.210), kind=kOutput, calls=%fused_computation.1 | convolution fusion | flops 1115676672 | bytes 70321152 | tf_op jit(solution)/shard_map/qhd,khd->hqk/dot_general | solution.py:167
  764.1 28.5 %multiply_convert_fusion = bf16[16,512,1024]{2,1,0:T(8,128)(2,1)} fusion(f32[16,512,1024]{2,1,0:T(8,128)} %get-tuple-element.101, f32[16,512,1024]{2,1,0:T(8,128)} %get-tuple-element.87, f32[16,512]{1,0:T(8,128)S(1)} %get-tuple-element.100, f32[16,512]{1,0:T(8,128)S(1)} %log_add_fusion, pred[1024]{0:T(1024)(128)(4,1)S(1)} %iota_compare_fusion), kind=kLoop, calls=%fused_computation | loop fusion | flops 50331648 | bytes 83952640 | tf_op jit(solution)/shard_map/convert_element_type | solution.py:174
  792.5 10.2 multiply_convert_fusion.4
  803.0 13.4 convert_reduce_fusion.9
  816.5 12.1 convert_reduce_fusion.5
  828.8 4.8 fusion.84
  838.1 5.4 convolution_add_fusion.2
  849.8 5.4 copy.70
  861.1 5.4 copy.74
  866.6 4.4 fusion.50
  871.0 5.7 add_bitcast_fusion.1
  876.8 5.4 copy.72
  882.9 16.0 fusion.87
  898.9 20.5 convolution_add_fusion.1
  920.1 13.5 fusion.104
  933.6 11.7 convolution_add_fusion
  946.1 39.8 %all-reduce = f32[4096]{0:T(1024)S(1)} all-reduce(f32[4096]{0:T(1024)S(1)} %add.343), channel_id=13, replica_groups=mesh['dp'=16,'seq'=2] {'dp','seq'}, use_global_device_ids=true, to_apply=%region_51.52.clone | all-reduce | flops 4096 | bytes 32768
  1002.9 102.6 %reduce-scatter.28.cloned.1.call-done = f32[32,1024]{1,0:T(8,128)} async-done(((f32[1024,1024]{1,0:T(8,128)}), f32[32,1024]{1,0:T(8,128)}) %reduce-scatter.28.cloned.1.call-update) | async-done | bytes 131088 | tf_op jit(solution)/shard_map/reduce_scatter | solution.py:234
  1105.5 141.5 %reduce-scatter.34.cloned.1.call-done = f32[32,1024]{1,0:T(8,128)} async-done(((f32[1024,1024]{1,0:T(8,128)}), f32[32,1024]{1,0:T(8,128)}) %reduce-scatter.34.cloned.1.call-update) | async-done | bytes 131088
  1247.0 140.9 %reduce-scatter.38.cloned.1.call-done = f32[32,1024]{1,0:T(8,128)} async-done(((f32[1024,1024]{1,0:T(8,128)}), f32[32,1024]{1,0:T(8,128)}) %reduce-scatter.38.cloned.1.call-update) | async-done | bytes 131088
  1387.8 141.6 %reduce-scatter.36.cloned.1.call-done = f32[32,1024]{1,0:T(8,128)} async-done(((f32[1024,1024]{1,0:T(8,128)}), f32[32,1024]{1,0:T(8,128)}) %reduce-scatter.36.cloned.1.call-update) | async-done | bytes 131088
  1529.5 360.9 %reduce-scatter.32.cloned.1.call-done = f32[128,1024]{1,0:T(8,128)} async-done(((f32[4096,1024]{1,0:T(8,128)}), f32[128,1024]{1,0:T(8,128)}) %reduce-scatter.32.cloned.1.call-update) | async-done | bytes 524304 | tf_op jit(solution)/shard_map/reduce_scatter | solution.py:236
  1890.3 361.5 %reduce-scatter.30.cloned.1.call-done = f32[32,4096]{1,0:T(8,128)} async-done(((f32[1024,4096]{1,0:T(8,128)}), f32[32,4096]{1,0:T(8,128)}) %reduce-scatter.30.cloned.1.call-update) | async-done | bytes 524304 | tf_op jit(solution)/shard_map/reduce_scatter | solution.py:235
  (276 shorter events, 70.6 us)
Async XLA Ops:
  7.2 64.5 %all-gather.13.cloned.1.call-start = ((), (), s32[]{:S(2)}) async-start(), calls=%async_computation.11 | async-start | bytes 2162688 | tf_op jit(solution)/shard_map/all_gather | solution.py:18
  7.9 119.9 %all-gather.19.cloned.1.call-start = ((), (), s32[]{:S(2)}) async-start(), calls=%async_computation.14 | async-start | bytes 2162688 | tf_op jit(solution)/shard_map/all_gather | solution.py:17
  8.7 193.1 %all-gather.17.cloned.1.call-start = ((), (), s32[]{:S(2)}) async-start(), calls=%async_computation.13 | async-start | bytes 2162688 | tf_op jit(solution)/shard_map/all_gather | solution.py:16
  9.4 209.5 %all-gather.29.cloned.1.call-start = ((), (), s32[]{:S(2)}) async-start(), calls=%async_computation.19 | async-start | bytes 3145728 | tf_op jit(solution)/shard_map/all_gather | solution.py:107
  71.6 489.1 %copy-start.43 = (f32[1,1024]{1,0:T(1,128)}, f32[1,1024]{1,0:T(1,128)S(1)}, u32[]{:S(2)}) copy-start(f32[1,1024]{1,0:T(1,128)S(1)} %get-tuple-element.75) | copy-start | bytes 12292
  71.6 568.8 %copy-start.41 = (f32[1,1024]{1,0:T(1,128)}, f32[1,1024]{1,0:T(1,128)S(1)}, u32[]{:S(2)}) copy-start(f32[1,1024]{1,0:T(1,128)S(1)} %get-tuple-element.76) | copy-start | bytes 12292
  76.0 177.5 %all-gather.15.cloned.1.call-start = ((), (), s32[]{:S(2)}) async-start(), calls=%async_computation.12 | async-start | bytes 3145728 | tf_op jit(solution)/shard_map/all_gather | solution.py:107
  79.9 208.1 %all-gather.31.cloned.1.call-start = ((), (), s32[]{:S(2)}) async-start(), calls=%async_computation.20 | async-start | bytes 3145728 | tf_op jit(solution)/shard_map/all_gather | solution.py:106
  131.7 6.7 copy-start.76
  131.7 190.9 %all-gather.21.cloned.1.call-start = ((), (), s32[]{:S(2)}) async-start(), calls=%async_computation.15 | async-start | bytes 3145728 | tf_op jit(solution)/shard_map/all_gather | solution.py:106
  135.7 248.1 %all-gather.23.cloned.1.call-start = ((), (), s32[]{:S(2)}) async-start(), calls=%async_computation.16 | async-start | bytes 2162688 | tf_op jit(solution)/shard_map/all_gather | solution.py:19
  136.4 326.7 %all-gather.25.cloned.1.call-start = ((), (), s32[]{:S(2)}) async-start(), calls=%async_computation.17 | async-start | bytes 8650752 | tf_op jit(solution)/shard_map/all_gather | solution.py:20
  137.2 405.0 %all-gather.27.cloned.1.call-start = ((), (), s32[]{:S(2)}) async-start(), calls=%async_computation.18 | async-start | bytes 8650752 | tf_op jit(solution)/shard_map/all_gather | solution.py:21
  137.8 695.9 %reduce-scatter.22.cloned.1.call-start = ((), (), s32[]{:S(2)}) async-start(), calls=%async_computation.22 | async-start | bytes 3145728 | tf_op jit(solution)/shard_map/reduce_scatter | solution.py:194
  198.6 406.7 %copy-start.64 = (f32[32,1,128]{2,1,0:T(1,128)}, f32[32,1,128]{2,1,0:T(1,128)S(1)}, u32[]{:S(2)}) copy-start(f32[32,1,128]{2,1,0:T(1,128)S(1)} %convert_element_type.307) | copy-start | bytes 49156
  199.3 157.3 %copy-start.47 = (pred[1024]{0:T(1024)(128)(4,1)}, pred[1024]{0:T(1024)(128)(4,1)S(1)}, u32[]{:S(2)}) copy-start(pred[1024]{0:T(1024)(128)(4,1)S(1)} %iota_compare_fusion.1) | copy-start | bytes 3076
  207.3 181.7 %copy-start.7 = (bf16[512,1024]{0,1:T(8,128)(2,1)}, bf16[512,1024]{0,1:T(8,128)(2,1)S(1)}, u32[]{:S(2)}) copy-start(bf16[512,1024]{0,1:T(8,128)(2,1)S(1)} %copy.61) | copy-start | bytes 3145732
  290.8 98.1 %copy-start.2 = (bf16[1024,1024]{0,1:T(8,128)(2,1)}, bf16[1024,1024]{0,1:T(8,128)(2,1)S(1)}, u32[]{:S(2)}) copy-start(bf16[1024,1024]{0,1:T(8,128)(2,1)S(1)} %copy.62) | copy-start | bytes 6291460
  356.6 15.8 copy-start.39
  387.3 234.4 %copy-start.66 = (f32[512]{0:T(512)}, f32[512]{0:T(512)S(1)}, u32[]{:S(2)}) copy-start(f32[512]{0:T(512)S(1)} %broadcast_multiply_fusion.11) | copy-start | bytes 6148
  402.5 14.8 copy-start.10
  435.2 205.2 %copy-start = (f32[512,1024]{1,0:T(8,128)}, f32[512,1024]{1,0:T(8,128)S(1)}, u32[]{:S(2)}) copy-start(f32[512,1024]{1,0:T(8,128)S(1)} %get-tuple-element.89) | copy-start | bytes 6291460
  435.2 205.2 %copy-start.45 = (f32[512]{0:T(512)}, f32[512]{0:T(512)S(1)}, u32[]{:S(2)}) copy-start(f32[512]{0:T(512)S(1)} %broadcast_multiply_fusion.9) | copy-start | bytes 6148
  435.6 186.1 %copy-start.73 = (f32[512]{0:T(512)}, f32[512]{0:T(512)S(1)}, u32[]{:S(2)}) copy-start(f32[512]{0:T(512)S(1)} %add_rsqrt_fusion.3) | copy-start | bytes 6148
  435.6 204.8 %copy-start.50 = (f32[512]{0:T(512)}, f32[512]{0:T(512)S(1)}, u32[]{:S(2)}) copy-start(f32[512]{0:T(512)S(1)} %add_rsqrt_fusion.1) | copy-start | bytes 6148
  542.2 11.5 copy-start.77
  553.7 7.1 copy-start.78
  577.9 15.5 copy-start.35
  577.9 27.4 %copy-start.33 = (f32[512,1024]{1,0:T(8,128)}, f32[512,1024]{1,0:T(8,128)S(1)}, u32[]{:S(2)}) copy-start(f32[512,1024]{1,0:T(8,128)S(1)} %get-tuple-element.60) | copy-start | bytes 6291460
  577.9 15.5 copy-start.17
  593.4 11.9 copy-start.82
  621.7 14.6 copy-start.20
  662.1 173.2 %reduce-scatter.26.cloned.1.call-start = ((), (), s32[]{:S(2)}) async-start(), calls=%async_computation.24 | async-start | bytes 3145728 | tf_op jit(solution)/shard_map/reduce_scatter | solution.py:194
  662.2 16.0 copy-start.12
  701.6 165.0 %reduce-scatter.20.cloned.1.call-start = ((), (), s32[]{:S(2)}) async-start(), calls=%async_computation.21 | async-start | bytes 3145728 | tf_op jit(solution)/shard_map/reduce_scatter | solution.py:188
  701.7 28.9 %copy-start.9 = (bf16[512,1024]{0,1:T(8,128)(2,1)S(1)}, bf16[512,1024]{0,1:T(8,128)(2,1)}, u32[]{:S(2)}) copy-start(bf16[512,1024]{0,1:T(8,128)(2,1)} %copy.58) | copy-start | bytes 3145732
  730.5 10.3 copy-start.11
  764.0 107.0 %reduce-scatter.24.cloned.1.call-start = ((), (), s32[]{:S(2)}) async-start(), calls=%async_computation.23 | async-start | bytes 3145728 | tf_op jit(solution)/shard_map/reduce_scatter | solution.py:188
  764.1 28.5 %copy-start.8 = (bf16[512,1024]{0,1:T(8,128)(2,1)S(1)}, bf16[512,1024]{0,1:T(8,128)(2,1)}, u32[]{:S(2)}) copy-start(bf16[512,1024]{0,1:T(8,128)(2,1)} %copy-done.7) | copy-start | bytes 3145732
  802.7 13.8 copy-start.3
  802.7 198.8 %reduce-scatter.40.cloned.1.call-start = ((), (), s32[]{:S(2)}) async-start(), calls=%async_computation.31 | async-start | bytes 540672
  816.5 12.2 copy-start.24
  828.7 6.5 copy-start.60
  828.8 6.5 copy-start.70
  828.8 6.5 copy-start.71
  828.8 8.0 copy-start.55
  828.8 8.0 copy-start.56
  828.8 8.0 copy-start.57
  828.8 8.0 copy-start.61
  828.8 8.0 copy-start.68
  828.8 8.0 copy-start.69
  838.0 267.5 %reduce-scatter.28.cloned.1.call-start = ((), (), s32[]{:S(2)}) async-start(), calls=%async_computation.25 | async-start | bytes 4325376 | tf_op jit(solution)/shard_map/reduce_scatter | solution.py:234
  843.5 403.5 %reduce-scatter.34.cloned.1.call-start = ((), (), s32[]{:S(2)}) async-start(), calls=%async_computation.28 | async-start | bytes 4325376
  855.3 532.6 %reduce-scatter.38.cloned.1.call-start = ((), (), s32[]{:S(2)}) async-start(), calls=%async_computation.30 | async-start | bytes 4325376
  866.5 662.9 %reduce-scatter.36.cloned.1.call-start = ((), (), s32[]{:S(2)}) async-start(), calls=%async_computation.29 | async-start | bytes 4325376
  882.2 16.7 copy-start.34
  882.2 1008.1 %reduce-scatter.32.cloned.1.call-start = ((), (), s32[]{:S(2)}) async-start(), calls=%async_computation.27 | async-start | bytes 17301504 | tf_op jit(solution)/shard_map/reduce_scatter | solution.py:236
  919.4 14.2 copy-start.1
  919.5 14.2 copy-start.46
  919.5 14.1 copy-start.51
  919.5 1332.3 %reduce-scatter.30.cloned.1.call-start = ((), (), s32[]{:S(2)}) async-start(), calls=%async_computation.26 | async-start | bytes 17301504 | tf_op jit(solution)/shard_map/reduce_scatter | solution.py:235
  920.1 13.5 copy-start.25
  945.4 41.1 %copy-start.28 = (bf16[1,512,1024]{2,1,0:T(8,128)(2,1)S(1)}, bf16[1,512,1024]{2,1,0:T(8,128)(2,1)}, u32[]{:S(2)}) copy-start(bf16[1,512,1024]{2,1,0:T(8,128)(2,1)} %get-tuple-element.68) | copy-start | bytes 3145732
  945.4 41.1 %copy-start.29 = (bf16[1,512,1024]{2,1,0:T(8,128)(2,1)S(1)}, bf16[1,512,1024]{2,1,0:T(8,128)(2,1)}, u32[]{:S(2)}) copy-start(bf16[1,512,1024]{2,1,0:T(8,128)(2,1)} %get-tuple-element.69) | copy-start | bytes 3145732
  (40 other events, 92.2 us)
Sparse Core Ops, SparseCore 0:
  11.1 58.1 all-gather.12
  72.4 55.3 all-gather.18
  130.9 55.3 all-gather.16
  188.3 30.5 all-gather.28
  220.3 33.0 all-gather.14
  254.8 33.1 all-gather.30
  289.5 33.1 all-gather.20
  325.8 57.9 all-gather.22
  386.8 76.2 all-gather.24
  466.1 75.9 all-gather.26
  662.3 28.9 reduce-scatter.21
  701.7 28.9 reduce-scatter.25
  764.1 29.2 reduce-scatter.19
  802.9 29.5 reduce-scatter.23
  838.1 124.5 reduce-scatter.39
  965.5 139.9 reduce-scatter.27
  1108.3 138.6 reduce-scatter.33
  1249.8 138.0 reduce-scatter.37
  1390.8 138.6 reduce-scatter.35
  1532.3 357.9 reduce-scatter.31
  1893.3 358.4 reduce-scatter.29
where the time goes:
time: 2270 us; the launch traced here: 2260 us
  waiting for transfers between devices  1510 us (67%)
  matrix products  414 us (18%)
  blocking collectives  161 us (7%)
  other arithmetic  108 us (5%)
  local copies, waits for them, and re-layouts  53.1 us (2%)
    unnamed x25, waiting for transfers between devices  428 us
    reduce_scatter x1, waiting for transfers between devices, per_device(): lax.psum_scatter(sums[4], ('dp', 'seq'), scatter_dimension=0, tiled=True)  361 us
    reduce_scatter x1, waiting for transfers between devices, per_device(): lax.psum_scatter(sums[5], ('dp', 'seq'), scatter_dimension=0, tiled=True)  361 us
    reduce_scatter x1, waiting for transfers between devices, per_device(): lax.psum_scatter(sums[3], ('dp', 'seq'), scatter_dimension=0, tiled=True)  103 us
    all_gather x1, waiting for transfers between devices, fetch_forward(): lax.all_gather(w_down, ('dp', 'seq'), axis=0, tiled=True)  67.1 us
    all_gather x2, waiting for transfers between devices, per_device(): lax.all_gather(keys_own, 'seq', axis=0, tiled=True)  62.4 us
    all_gather x1, blocking collectives, fetch_forward(): lax.all_gather(vectors, ('dp', 'seq'), axis=1, tiled=True)  61.5 us
    all_gather x1, blocking collectives, fetch_forward(): lax.all_gather(up_bias, ('dp', 'seq'), axis=0, tiled=True)  60.2 us
  transfers between devices with their start and end apart: 21, of which 14 were waited for; matrix products, arithmetic and copies ran while one was open for 20% of the time, Pallas kernels for 0%

commit v1 on v0

--- a/solution.py
+++ b/solution.py
@@ -1,8 +1,11 @@
+import functools
 import math
 
 import jax
 import jax.numpy as jnp
 from jax import lax
+from jax.experimental import pallas as pl
+from jax.experimental.pallas import tpu as pltpu
 from jax.sharding import PartitionSpec as P
 
 H = 16
@@ -253,6 +256,889 @@
     )
 
 
+MESH = pl.DeviceIdType.MESH
+F32 = jnp.float32
+BF16 = jnp.bfloat16
+ANY = pl.ANY
+VMEM = pltpu.VMEM
+LOG2E = math.log2(math.e)
+LIMIT = 58 * 1024 * 1024
+GELU_C = math.sqrt(2.0 / math.pi)
+GELU_A = 0.044715
+
+
+def nt(a, b):
+    return lax.dot_general(a, b, (((1,), (1,)), ((), ())), preferred_element_type=F32)
+
+
+def nn(a, b):
+    return lax.dot_general(a, b, (((1,), (0,)), ((), ())), preferred_element_type=F32)
+
+
+def tn(a, b):
+    return lax.dot_general(a, b, (((0,), (0,)), ((), ())), preferred_element_type=F32)
+
+
+def place():
+    dp = lax.axis_index("dp")
+    return dp // 4, (dp // 2) % 2, dp % 2, lax.axis_index("seq")
+
+
+def device(z, x, c, y):
+    return (z * 4 + x * 2 + c, y)
+
+
+def greet(z, x, c, y):
+    barrier = pltpu.get_barrier_semaphore()
+    partners = [device(z, x, 1 - c, y), device(z, 1 - x, c, y), device(z, x, c, 1 - y)]
+    partners += [device((z + d) % 4, x, c, y) for d in (1, 2, 3)]
+    for partner in partners:
+        pl.semaphore_signal(barrier, inc=1, device_id=partner, device_id_type=MESH)
+    pl.semaphore_wait(barrier, len(partners))
+
+
+def gather_copies(ref, send, recv, order, phase, pos):
+    z, x, c, y = pos
+    every = slice(None)
+
+    def copy(region, slot, target):
+        return pltpu.make_async_remote_copy(
+            src_ref=ref.at[region],
+            dst_ref=ref.at[region],
+            send_sem=send.at[slot],
+            recv_sem=recv.at[slot],
+            device_id=device(*target),
+            device_id_type=MESH,
+        )
+
+    done = order[:phase]
+    have = (
+        every if "z" in done else z,
+        every if "x" in done else x,
+        every if "c" in done else c,
+        every if "y" in done else y,
+    )
+    axis = order[phase]
+    if axis == "z":
+        return [copy(have, 2 + d, ((z + d) % 4, x, c, y)) for d in (1, 2, 3)]
+    if axis == "x":
+        return [copy(have, 0, (z, 1 - x, c, y))]
+    if axis == "y":
+        return [copy(have, 1, (z, x, c, 1 - y))]
+    return [copy(have, 2, (z, x, 1 - c, y))]
+
+
+ORDERS = ("yzxc", "zxyc")
+PHASES = 4
+SLOTS = 6
+
+
+def gather_phase(ref, send, recv, phase, pos):
+    for core, order in enumerate(ORDERS):
+
+        @pl.when(pos[2] == core)
+        def _():
+            if phase > 0:
+                for copy in gather_copies(ref, send, recv, order, phase - 1, pos):
+                    copy.wait_recv()
+            if phase < PHASES:
+                for copy in gather_copies(ref, send, recv, order, phase, pos):
+                    copy.start()
+
+
+def gather_sent(ref, send, recv, pos):
+    for core, order in enumerate(ORDERS):
+
+        @pl.when(pos[2] == core)
+        def _():
+            for phase in range(PHASES):
+                for copy in gather_copies(ref, send, recv, order, phase, pos):
+                    copy.wait_send()
+
+
+def gather_kernel(ws, sm, tok, cot, wf, sf, xs, ct, send, recv, own, tsend, trecv):
+    pos = place()
+    z, x, c, y = pos
+    chunks = ws.shape[0]
+    copies = [
+        pltpu.make_async_copy(ws, wf.at[:, z, x, c, y], own.at[0]),
+        pltpu.make_async_copy(sm, sf.at[z, x, c, y], own.at[1]),
+        pltpu.make_async_copy(tok.at[y, 0], xs.at[0], own.at[2]),
+        pltpu.make_async_copy(cot.at[y, 0], ct.at[0], own.at[3]),
+    ]
+    for copy in copies:
+        copy.start()
+    greet(*pos)
+    swaps = []
+    for index, (src, dst) in enumerate(((tok, xs), (cot, ct))):
+        swaps.append(
+            pltpu.make_async_remote_copy(
+                src_ref=src.at[1 - y, 0],
+                dst_ref=dst.at[1],
+                send_sem=tsend.at[index],
+                recv_sem=trecv.at[index],
+                device_id=device(z, x, c, 1 - y),
+                device_id_type=MESH,
+            )
+        )
+    swaps[0].start()
+    copies[0].wait()
+    copies[1].wait()
+
+    def chunk(index):
+        return (wf.at[index], send.at[index], recv.at[index])
+
+    small = (sf, send.at[chunks], recv.at[chunks])
+
+    def step(t, carry):
+        for phase in range(PHASES + 1):
+            index = t - phase
+
+            @pl.when((index >= 0) & (index < chunks))
+            def _():
+                gather_phase(*chunk(index), phase, pos)
+
+            @pl.when(index == 0)
+            def _():
+                gather_phase(*small, phase, pos)
+
+        return carry
+
+    lax.fori_loop(0, chunks + PHASES, step, 0)
+    swaps[1].start()
+    for copy in copies[2:]:
+        copy.wait()
+    gather_sent(*small, pos)
+
+    def finish(index, carry):
+        gather_sent(*chunk(index), pos)
+        return carry
+
+    lax.fori_loop(0, chunks, finish, 0)
+    for swap in swaps:
+        swap.wait()
+
+
+def gather(ws, sm, tok, cot):
+    chunks, rows, width = ws.shape
+    half = tok.shape[2]
+    return pl.pallas_call(
+        gather_kernel,
+        out_shape=(
+            jax.ShapeDtypeStruct((chunks, 4, 2, 2, 2, rows, width), BF16),
+            jax.ShapeDtypeStruct((4, 2, 2, 2) + sm.shape, BF16),
+            jax.ShapeDtypeStruct((2, half, width), BF16),
+            jax.ShapeDtypeStruct((2, half, width), BF16),
+        ),
+        in_specs=[pl.BlockSpec(memory_space=ANY)] * 4,
+        out_specs=[pl.BlockSpec(memory_space=ANY)] * 4,
+        scratch_shapes=[
+            pltpu.SemaphoreType.DMA((chunks + 1, SLOTS)),
+            pltpu.SemaphoreType.DMA((chunks + 1, SLOTS)),
+            pltpu.SemaphoreType.DMA((4,)),
+            pltpu.SemaphoreType.DMA((2,)),
+            pltpu.SemaphoreType.DMA((2,)),
+        ],
+        compiler_params=pltpu.CompilerParams(collective_id=0, has_side_effects=True),
+        name="gather",
+    )(ws, sm, tok, cot)
+
+
+def scatter_copies(core, phase, grad, bufs, send, recv, pos):
+    z, x, c, y = pos
+    b0, b1, b2, b3 = bufs
+
+    def remote(src, dst, slot, target):
+        return pltpu.make_async_remote_copy(
+            src_ref=src,
+            dst_ref=dst,
+            send_sem=send.at[slot],
+            recv_sem=recv.at[slot],
+            device_id=device(*target),
+            device_id_type=MESH,
+        )
+
+    if phase == 0:
+        return [remote(grad.at[:, :, 1 - c], b0, 2, (z, x, 1 - c, y))]
+    if core == 0:
+        if phase == 1:
+            return [remote(b0.at[:, 1 - x], b1, 0, (z, 1 - x, c, y))]
+        if phase == 2:
+            return [
+                remote(b1.at[(z + d) % 4], b2.at[pl.ds(2 * (d - 1), 2)], 2 + d, ((z + d) % 4, x, c, y))
+                for d in (1, 2, 3)
+            ]
+        return [remote(b1.at[z, 1 - y], b3.at[0], 1, (z, x, c, 1 - y))]
+    if phase == 1:
+        return [remote(b0.at[:, :, 1 - y], b1, 1, (z, x, c, 1 - y))]
+    if phase == 2:
+        return [remote(b1.at[:, 1 - x], b2.at[pl.ds(0, 4)], 0, (z, 1 - x, c, y))]
+    return [remote(b2.at[(z + d) % 4], b3.at[d - 1], 2 + d, ((z + d) % 4, x, c, y)) for d in (1, 2, 3)]
+
+
+def scatter_add(core, phase, own, bufs, out, pos):
+    z, x, c, y = pos
+    b0, b1, b2, b3 = bufs
+
+    def plus(dst, a, b):
+        dst[...] = (a.astype(F32) + b.astype(F32)).astype(dst.dtype)
+
+    if phase == 0:
+        for zz in range(4):
+            for xx in range(2):
+                plus(b0.at[zz, xx], own[zz, xx], b0[zz, xx])
+    elif phase == 1:
+        for zz in range(4):
+            plus(b1.at[zz], b0[zz, x] if core == 0 else b0[zz, :, y], b1[zz])
+    elif core == 0:
+        if phase == 2:
+            total = b1[z].astype(F32)
+            for d in range(3):
+                total = total + b2[pl.ds(2 * d, 2)].astype(F32)
+            b1[z] = total.astype(BF16)
+        else:
+            out[...] = b1[z, y].astype(F32) + b3[0].astype(F32)
+    elif phase == 2:
+        for zz in range(4):
+            plus(b2.at[zz], b1[zz, x], b2[zz])
+    else:
+        total = b2[z].astype(F32)
+        for d in range(3):
+            total = total + b3[d].astype(F32)
+        out[...] = total
+
+
+def scatter_phase(phase, grad, own, own_sem, bufs, out, send, recv, pos):
+    c = pos[2]
+    mine = pltpu.make_async_copy(grad.at[:, :, c], own, own_sem)
+    if phase == 0:
+        mine.start()
+    if phase == 1:
+        mine.wait()
+    for core in (0, 1):
+
+        @pl.when(c == core)
+        def _():
+            if phase > 0:
+                for copy in scatter_copies(core, phase - 1, grad, bufs, send, recv, pos):
+                    copy.wait_recv()
+                scatter_add(core, phase - 1, own, bufs, out, pos)
+            if phase < PHASES:
+                for copy in scatter_copies(core, phase, grad, bufs, send, recv, pos):
+                    copy.start()
+
+
+def scatter_sent(grad, bufs, send, recv, pos):
+    for core in (0, 1):
+
+        @pl.when(pos[2] == core)
+        def _():
+            for phase in range(PHASES):
+                for copy in scatter_copies(core, phase, grad, bufs, send, recv, pos):
+                    copy.wait_send()
+
+
+def scatter_kernel(parts, *refs):
+    count = len(parts) + 1
+    grads, rows_ref = refs[:count], refs[count]
+    outs, small_out, rows_out = refs[count + 1 : 2 * count], refs[2 * count], refs[2 * count + 1]
+    bufs, small_bufs = refs[2 * count + 2 : 2 * count + 6], refs[2 * count + 6 : 2 * count + 10]
+    own, small_own, send, recv, own_sem, swap_sem = refs[2 * count + 10 :]
+    pos = place()
+    z, x, c, y = pos
+    greet(*pos)
+    swap = pltpu.make_async_remote_copy(
+        src_ref=rows_ref,
+        dst_ref=rows_out,
+        send_sem=swap_sem.at[0],
+        recv_sem=swap_sem.at[1],
+        device_id=device(z, x, c, 1 - y),
+        device_id_type=MESH,
+    )
+    swap.start()
+    total = sum(parts)
+    small = total
+    starts = [sum(parts[:k]) for k in range(len(parts))]
+
+    def view(index):
+        return [buf.at[index] for buf in bufs]
+
+    def step(t, carry):
+        for phase in range(PHASES + 1):
+            index = t - phase
+            for k, start in enumerate(starts):
+
+                @pl.when((index >= start) & (index < start + parts[k]))
+                def _():
+                    scatter_phase(
+                        phase,
+                        grads[k].at[index - start],
+                        own.at[index % 2],
+                        own_sem.at[index % 2],
+                        view(index),
+                        outs[k].at[index - start],
+                        send.at[index],
+                        recv.at[index],
+                        pos,
+                    )
+
+            @pl.when(index == total)
+            def _():
+                scatter_phase(
+                    phase,
+                    grads[-1],
+                    small_own,
+                    own_sem.at[2],
+                    small_bufs,
+                    small_out,
+                    send.at[small],
+                    recv.at[small],
+                    pos,
+                )
+
+        return carry
+
+    lax.fori_loop(0, total + 1 + PHASES, step, 0)
+    scatter_sent(grads[-1], small_bufs, send.at[small], recv.at[small], pos)
+
+    def finish(index, carry):
+        scatter_sent(grads[0].at[0], view(index), send.at[index], recv.at[index], pos)
+        return carry
+
+    lax.fori_loop(0, total, finish, 0)
+    swap.wait()
+
+
+def scatter(grads, small, rows_back, cid):
+    parts = [grad.shape[0] for grad in grads]
+    rows, width = grads[0].shape[-2:]
+    total = sum(parts)
+
+    def buffers(lead, rows, width):
+        return [
+            VMEM(lead + (4, 2, 2, rows, width), BF16),
+            VMEM(lead + (4, 2, rows, width), BF16),
+            VMEM(lead + (6, rows, width), BF16),
+            VMEM(lead + (3, rows, width), BF16),
+        ]
+
+    srows, swidth = small.shape[-2:]
+    return pl.pallas_call(
+        functools.partial(scatter_kernel, parts),
+        out_shape=[jax.ShapeDtypeStruct((n, rows, width), F32) for n in parts]
+        + [jax.ShapeDtypeStruct((srows, swidth), F32), jax.ShapeDtypeStruct(rows_back.shape, rows_back.dtype)],
+        in_specs=[pl.BlockSpec(memory_space=ANY)] * (len(parts) + 2),
+        out_specs=[pl.BlockSpec(memory_space=VMEM)] * (len(parts) + 1) + [pl.BlockSpec(memory_space=ANY)],
+        scratch_shapes=buffers((total,), rows, width)
+        + buffers((), srows, swidth)
+        + [
+            VMEM((2, 4, 2, 2, rows, width), BF16),
+            VMEM((4, 2, 2, srows, swidth), BF16),
+            pltpu.SemaphoreType.DMA((total + 1, SLOTS)),
+            pltpu.SemaphoreType.DMA((total + 1, SLOTS)),
+            pltpu.SemaphoreType.DMA((3,)),
+            pltpu.SemaphoreType.DMA((2,)),
+        ],
+        compiler_params=pltpu.CompilerParams(collective_id=cid, has_side_effects=True, vmem_limit_bytes=LIMIT),
+        name="scatter",
+    )(*grads, small, rows_back)
+
+
+def lanes(shape):
+    return lax.broadcasted_iota(jnp.int32, shape, len(shape) - 1)
+
+
+def attend_kernel(xs, wf, sf, kaug, qs, ks, vs, ctx, aug, res, vec, wbuf, wsem):
+    rows, width = xs.shape
+    block = 256
+    loads = [pltpu.make_async_copy(wf.at[i], wbuf.at[i % 2], wsem.at[i % 2]) for i in range(4)]
+    loads[0].start()
+    for g in range(8):
+        tile = sf[4 * g].astype(F32)
+        for s in range(1, 4):
+            tile = tile + sf[4 * g + s].astype(F32)
+        vec[0:8, 128 * g : 128 * g + 128] = tile[0:8]
+    for r in range(4):
+        for g in range(8):
+            vec[8 + r : 9 + r, 128 * g : 128 * g + 128] = sf[8 * r + g].astype(F32)[8:9]
+    for i, dst in enumerate((qs, ks, vs)):
+        loads[i].wait()
+        loads[i + 1].start()
+
+        def project(b, carry):
+            sl = pl.ds(pl.multiple_of(b * block, block), block)
+            out = nn(xs[sl, :], wbuf[i % 2])
+            if i == 0:
+                out = (out + vec[0:1, :]) * (LOG2E / 8.0)
+            elif i == 2:
+                out = out + vec[1:2, :]
+            dst[sl, :] = out.astype(BF16)
+            return carry
+
+        lax.fori_loop(0, rows // block, project, 0)
+
+    low1 = (lanes((1, 128)) < 64).astype(F32).astype(BF16)
+    high1 = (lanes((1, 128)) >= 64).astype(F32).astype(BF16)
+    ones1 = (lanes((1, 128)) % 64 == 0).astype(F32).astype(BF16)
+    qlane = lanes((block, 128))
+    sixty = qlane % 64
+
+    def pair(hp, carry):
+        cols = pl.ds(pl.multiple_of(hp * 128, 128), 128)
+        k2 = ks[:, cols]
+        v2 = vs[:, cols]
+        ka = k2 * low1 + kaug[...] * high1
+        kb = k2 * high1 + kaug[...] * low1
+
+        def query_block(b, carry):
+            sl = pl.ds(pl.multiple_of(b * block, block), block)
+            q2 = qs[sl, cols]
+            parts = []
+            for mine, other, kk in ((low1, high1, ka), (high1, low1, kb)):
+                s = nt(q2 * mine + ones1 * other, kk)
+                top = jnp.max(s, axis=1, keepdims=True)
+                e = jnp.exp2(s - top)
+                total = jnp.sum(e, axis=1, keepdims=True)
+                o = nn(e.astype(BF16), v2)
+                parts.append((o / total, -(top + jnp.log2(total))))
+            low = qlane < 64
+            ctx[sl, cols] = jnp.where(low, parts[0][0], parts[1][0]).astype(BF16)
+            neg = jnp.where(low, parts[1][1], parts[0][1])
+            hi = neg.astype(BF16).astype(F32)
+            mid = (neg - hi).astype(BF16).astype(F32)
+            lo = neg - hi - mid
+            aug[hp, sl, :] = jnp.where(
+                sixty == 0,
+                1.0,
+                jnp.where(sixty == 1, hi, jnp.where(sixty == 2, mid, jnp.where(sixty == 3, lo, 0.0))),
+            ).astype(BF16)
+            return carry
+
+        lax.fori_loop(0, rows // block, query_block, 0)
+        return carry
+
+    lax.fori_loop(0, width // 128, pair, 0)
+    loads[3].wait()
+
+    def project_out(b, carry):
+        sl = pl.ds(pl.multiple_of(b * block, block), block)
+        out = nn(ctx[sl, :], wbuf[1])
+        res[sl, :] = xs[sl, :].astype(F32) + (out + vec[2:3, :])
+        return carry
+
+    lax.fori_loop(0, rows // block, project_out, 0)
+
+
+def attend(xs, wf, sf, kaug):
+    rows, width = xs.shape
+    low = jax.ShapeDtypeStruct((rows, width), BF16)
+    return pl.pallas_call(
+        attend_kernel,
+        out_shape=(
+            low,
+            low,
+            low,
+            low,
+            jax.ShapeDtypeStruct((width // 128, rows, 128), BF16),
+            jax.ShapeDtypeStruct((rows, width), F32),
+            jax.ShapeDtypeStruct((16, width), F32),
+        ),
+        in_specs=[
+            pl.BlockSpec(memory_space=VMEM),
+            pl.BlockSpec(memory_space=ANY),
+            pl.BlockSpec(memory_space=VMEM),
+            pl.BlockSpec(memory_space=VMEM),
+        ],
+        out_specs=[pl.BlockSpec(memory_space=VMEM)] * 7,
+        scratch_shapes=[VMEM((2, width, width), BF16), pltpu.SemaphoreType.DMA((2,))],
+        compiler_params=pltpu.CompilerParams(vmem_limit_bytes=LIMIT),
+        cost_estimate=pl.CostEstimate(flops=2 * 6 * rows * width * width, bytes_accessed=30 << 20, transcendentals=1 << 24),
+        name="attend",
+    )(xs, wf, sf, kaug)
+
+
+def feed_kernel(res, ct, valid, vec, wu, wd, act, gres1, gwu, gwd, rows_out, bias_out, hid, acc, low, gdn, actv, slope):
+    step = pl.program_id(0)
+    chunks = pl.num_programs(0) // 2
+    rows, width = res.shape
+    block = 256
+    nb = rows // block
+    wide = wu.shape[1]
+    last = step == 2 * chunks - 1
+    down = jnp.concatenate([wd[jj, s] for s in range(4) for jj in range(4)], axis=0)
+
+    def blocks(body):
+        def run(b, carry):
+            body(b, pl.ds(pl.multiple_of(b * block, block), block))
+            return carry
+
+        lax.fori_loop(0, nb, run, 0)
+
+    def norm(v):
+        center = v - jnp.mean(v, axis=-1, keepdims=True)
+        inverse = lax.rsqrt(jnp.mean(center * center, axis=-1, keepdims=True) + 1e-05)
+        return center * inverse, inverse
+
+    def norm_back(g, normed, inverse, gain):
+        gn = g * gain
+        inner = gn - jnp.mean(gn, axis=-1, keepdims=True) - normed * jnp.mean(gn * normed, axis=-1, keepdims=True)
+        return inner * inverse
+
+    def rowsum(v):
+        return jnp.sum(v, axis=0, keepdims=True)
+
+    @pl.when(step == 0)
+    def _():
+        rows_out[...] = jnp.zeros_like(rows_out)
+
+        def body(b, sl):
+            normed, _ = norm(res[sl, :])
+            hidden = normed * vec[3:4, :] + vec[4:5, :]
+            hid[sl, :] = hidden
+            low[sl, :] = hidden.astype(BF16)
+
+        blocks(body)
+
+    @pl.when(step < chunks)
+    def _():
+        bias = vec[pl.ds(8 + step // 2, 1), pl.ds(pl.multiple_of((step % 2) * wide, wide), wide)]
+
+        def body(b, sl):
+            up = nn(low[sl, :], wu[...]) + bias
+            square = up * up
+            t = jnp.tanh(up * (GELU_C + (GELU_C * GELU_A) * square))
+            half = 0.5 * up
+            a = (half + half * t).astype(BF16)
+            d = 0.5 + 0.5 * t + half * (1.0 - t * t) * (GELU_C + (3.0 * GELU_C * GELU_A) * square)
+            actv[step, sl, :] = a
+            slope[step, sl, :] = d.astype(BF16)
+            part = nn(a, down)
+
+            @pl.when(step == 0)
+            def _():
+                acc[sl, :] = part
+
+            @pl.when(step > 0)
+            def _():
+                acc[sl, :] += part
+
+        blocks(body)
+
+    @pl.when(step == chunks - 1)
+    def _():
+        def body(b, sl):
+            normed, inverse = norm(hid[sl, :] + (acc[sl, :] + vec[5:6, :]))
+            ok = valid[sl, 0:1]
+            act[sl, :] = ((normed * vec[6:7, :] + vec[7:8, :]) * ok).astype(BF16)
+            g = ct[sl, :].astype(F32) * ok
+            back = norm_back(g, normed, inverse, vec[6:7, :])
+            acc[sl, :] = back
+            gd = back.astype(BF16)
+            gdn[sl, :] = gd
+            rows_out[6:7, :] += rowsum(g * normed)
+            rows_out[7:8, :] += rowsum(g)
+            rows_out[5:6, :] += rowsum(gd.astype(F32))
+
+        blocks(body)
+
+    @pl.when(step >= chunks)
+    def _():
+        i = step - chunks
+        bias_out[...] = jnp.zeros_like(bias_out)
+
+        def body(b, sl):
+            ga = nt(gdn[sl, :], down)
+            gu = (slope[i, sl, :].astype(F32) * ga).astype(BF16)
+            slope[i, sl, :] = gu
+            bias_out[0:1, :] += rowsum(gu.astype(F32))
+            acc[sl, :] += nt(gu, wu[...])
+
+        blocks(body)
+        for q in range(wide // 128):
+            part = tn(actv[i, :, 128 * q : 128 * q + 128], gdn[...]).astype(BF16)
+            for jj in range(4):
+                gwd[jj, q] = part[32 * jj : 32 * jj + 32]
+        for q in range(width // 256):
+            gwu[0, 256 * q : 256 * q + 256, :] = tn(low[:, 256 * q : 256 * q + 256], slope[i]).astype(BF16)
+
+    @pl.when(last)
+    def _():
+        def body(b, sl):
+            normed, inverse = norm(res[sl, :])
+            g = acc[sl, :]
+            back = norm_back(g, normed, inverse, vec[3:4, :])
+            gres1[sl, :] = back
+            rows_out[3:4, :] += rowsum(g * normed)
+            rows_out[4:5, :] += rowsum(g)
+            rows_out[2:3, :] += rowsum(back.astype(BF16).astype(F32))
+
+        blocks(body)
+
+
+def feed(res, ct, valid, vec, wf):
+    rows, width = res.shape
+    wide = 512
+    chunks = 4 * width // wide
+    up_w = wf.reshape(12, width, width)
+    down_w = wf.reshape(12, 32, 32, width)
+
+    def whole(shape):
+        return pl.BlockSpec(shape, lambda i: (0,) * len(shape), pipeline_mode=pl.Buffered(1))
+
+    def second(i):
+        return jnp.maximum(i - chunks, 0)
+
+    return pl.pallas_call(
+        feed_kernel,
+        grid=(2 * chunks,),
+        out_shape=(
+            jax.ShapeDtypeStruct((rows, width), BF16),
+            jax.ShapeDtypeStruct((rows, width), F32),
+            jax.ShapeDtypeStruct((4, width, width), BF16),
+            jax.ShapeDtypeStruct((4, 32, 32, width), BF16),
+            jax.ShapeDtypeStruct((8, width), F32),
+            jax.ShapeDtypeStruct((chunks, 8, wide), F32),
+        ),
+        in_specs=[
+            whole((rows, width)),
+            whole((rows, width)),
+            whole((rows, 128)),
+            whole((16, width)),
+            pl.BlockSpec((None, width, wide), lambda i: (4 + (i % chunks) // 2, 0, i % 2)),
+            pl.BlockSpec((4, 4, 32, width), lambda i: (2, i % chunks, 0, 0)),
+        ],
+        out_specs=[
+            whole((rows, width)),
+            whole((rows, width)),
+            pl.BlockSpec((1, width, wide), lambda i: (second(i) // 2, 0, second(i) % 2)),
+            pl.BlockSpec((4, 4, 32, width), lambda i: (0, second(i), 0, 0)),
+            whole((8, width)),
+            pl.BlockSpec((None, 8, wide), lambda i: (second(i), 0, 0)),
+        ],
+        scratch_shapes=[
+            VMEM((rows, width), F32),
+            VMEM((rows, width), F32),
+            VMEM((rows, width), BF16),
+            VMEM((rows, width), BF16),
+            VMEM((chunks, rows, wide), BF16),
+            VMEM((chunks, rows, wide), BF16),
+        ],
+        compiler_params=pltpu.CompilerParams(vmem_limit_bytes=LIMIT, dimension_semantics=("arbitrary",)),
+        cost_estimate=pl.CostEstimate(flops=2 * 24 * rows * width * width, bytes_accessed=80 << 20, transcendentals=1 << 22),
+        name="feed",
+    )(res, ct, valid, vec, up_w, down_w)
+
+
+def retreat_kernel(gres1, xs, wf, qs, ks, vs, ctx, aug, kaug, gtok, dw, rows_out, gat, gcx, gqs, gks, gvs, wbuf, dbuf, wsem, dsem):
+    rows, width = xs.shape
+    block = 256
+    nb = rows // block
+    order = (3, 0, 1, 2)
+    loads = [pltpu.make_async_copy(wf.at[order[i]], wbuf.at[i % 2], wsem.at[i % 2]) for i in range(4)]
+    stores = [pltpu.make_async_copy(dbuf.at[i % 2], dw.at[order[i]], dsem.at[i % 2]) for i in range(4)]
+    loads[0].start()
+    rows_out[...] = jnp.zeros_like(rows_out)
+
+    def blocks(body):
+        def run(b, carry):
+            body(pl.ds(pl.multiple_of(b * block, block), block))
+            return carry
+
+        lax.fori_loop(0, nb, run, 0)
+
+    def weight_grad(slot, left, right):
+        def run(b, carry):
+            sl = pl.ds(pl.multiple_of(b * block, block), block)
+            dbuf[slot, sl, :] = tn(left[:, sl], right[...]).astype(BF16)
+            return carry
+
+        lax.fori_loop(0, width // block, run, 0)
+
+    def low_rows(sl):
+        gat[sl, :] = gres1[sl, :].astype(BF16)
+
+    blocks(low_rows)
+    loads[0].wait()
+    loads[1].start()
+
+    def context_rows(sl):
+        gcx[sl, :] = nt(gat[sl, :], wbuf[0]).astype(BF16)
+
+    blocks(context_rows)
+    weight_grad(0, ctx, gat)
+    stores[0].start()
+
+    low1 = (lanes((1, 128)) < 64).astype(F32).astype(BF16)
+    high1 = (lanes((1, 128)) >= 64).astype(F32).astype(BF16)
+    ones1 = (lanes((1, 128)) % 64 < 2).astype(F32).astype(BF16)
+    alane = lanes((rows, 128))
+    low = alane < 64
+    sixty = alane % 64
+
+    def pair(hp, carry):
+        cols = pl.ds(pl.multiple_of(hp * 128, 128), 128)
+        q2 = qs[:, cols]
+        g2 = gcx[:, cols]
+        au = aug[hp]
+        prod = g2.astype(F32) * ctx[:, cols].astype(F32)
+        da = -jnp.sum(jnp.where(low, prod, 0.0), axis=1, keepdims=True)
+        db = -jnp.sum(jnp.where(low, 0.0, prod), axis=1, keepdims=True)
+        neg = jnp.where(low, db, da)
+        hi = neg.astype(BF16).astype(F32)
+        daug = jnp.where(sixty == 0, hi, jnp.where(sixty == 1, neg - hi, 0.0)).astype(BF16)
+        qa = (q2 * low1 + au * high1, q2 * high1 + au * low1)
+        ga = (g2 * low1 + daug * high1, g2 * high1 + daug * low1)
+        gq = []
+        for head in range(2):
+            mine, other = (low1, high1) if head == 0 else (high1, low1)
+            total = jnp.zeros((128, rows), F32)
+            for b in range(nb):
+                sl = slice(b * block, (b + 1) * block)
+                k2 = ks[sl, cols]
+                v2 = vs[sl, cols]
+                s = nt(k2 * mine + kaug[sl, :] * other, qa[head])
+                p = jnp.exp2(s)
+                gp = nt(v2 * mine + ones1 * other, ga[head])
+                ds = (p * gp).astype(BF16)
+                gv = nn(p.astype(BF16), g2).astype(BF16)
+                gk = (nn(ds, q2) * (1.0 / LOG2E)).astype(BF16)
+                total = total + tn(k2, ds)
+                if head == 0:
+                    gvs[sl, cols] = gv
+                    gks[sl, cols] = gk
+                else:
+                    gvs[sl, cols] = gvs[sl, cols] * low1 + gv * high1
+                    gks[sl, cols] = gks[sl, cols] * low1 + gk * high1
+            gq.append(total)
+        both = jnp.concatenate([gq[0][0:64], gq[1][64:128]], axis=0) * 0.125
+        gqs[:, cols] = both.T.astype(BF16)
+        return carry
+
+    lax.fori_loop(0, width // 128, pair, 0)
+
+    for i, (left, base) in enumerate(((gqs, gres1), (gks, gtok), (gvs, gtok)), start=1):
+        loads[i].wait()
+        if i < 3:
+            loads[i + 1].start()
+
+        def token_rows(sl):
+            gtok[sl, :] = base[sl, :] + nt(left[sl, :], wbuf[i % 2])
+            if i != 2:
+                row = 0 if i == 1 else 1
+                rows_out[row : row + 1, :] += jnp.sum(left[sl, :].astype(F32), axis=0, keepdims=True)
+
+        blocks(token_rows)
+        if i >= 2:
+            stores[i - 2].wait()
+        weight_grad(i % 2, xs, left)
+        stores[i].start()
+    stores[2].wait()
+    stores[3].wait()
+
+
+def retreat(gres1, xs, wf, qs, ks, vs, ctx, aug, kaug):
+    rows, width = xs.shape
+    vmem = pl.BlockSpec(memory_space=VMEM)
+    hbm = pl.BlockSpec(memory_space=ANY)
+    return pl.pallas_call(
+        retreat_kernel,
+        out_shape=(
+            jax.ShapeDtypeStruct((rows, width), F32),
+            jax.ShapeDtypeStruct((4, width, width), BF16),
+            jax.ShapeDtypeStruct((8, width), F32),
+        ),
+        in_specs=[vmem, vmem, hbm] + [vmem] * 6,
+        out_specs=[vmem, hbm, vmem],
+        scratch_shapes=[VMEM((rows, width), BF16)] * 5
+        + [
+            VMEM((2, width, width), BF16),
+            VMEM((2, width, width), BF16),
+            pltpu.SemaphoreType.DMA((2,)),
+            pltpu.SemaphoreType.DMA((2,)),
+        ],
+        compiler_params=pltpu.CompilerParams(vmem_limit_bytes=LIMIT),
+        cost_estimate=pl.CostEstimate(flops=2 * 14 * rows * width * width, bytes_accessed=40 << 20, transcendentals=1 << 24),
+        name="retreat",
+    )(gres1, xs, wf, qs, ks, vs, ctx, aug, kaug)
+
+
+def paired(
+    tokens, lengths, w_query, w_key, w_value, w_out, w_up, w_down, vectors, up_bias, cotangent
+):
+    half, width = tokens.shape[2:]
+    rows = 2 * half
+    rank = lax.axis_index("dp") * 2 + lax.axis_index("seq")
+    y = lax.axis_index("seq")
+    shard = w_query.shape[0]
+    ws = jnp.concatenate(
+        [
+            jnp.stack([w_query, w_key, w_value, w_out]),
+            w_up.reshape(shard, 4, width).transpose(1, 0, 2),
+            w_down.reshape(4, shard, width),
+        ]
+    )
+    spot = jnp.tile(vectors, (1, 4)) * (jnp.arange(128) // 32 == rank % 4).astype(BF16)
+    sm = jnp.concatenate([spot, up_bias[None, :], jnp.zeros((7, 128), BF16)])
+    wf, sf, xs, ct = gather(ws, sm, tokens, cotangent)
+    xs = xs.reshape(rows, width)
+    ct = ct.reshape(rows, width)
+    wsquare = wf.reshape(12, width, width)
+    length = lax.dynamic_index_in_dim(lengths[:, 0], y, keepdims=False)
+    near = jnp.arange(half, dtype=jnp.int32)
+    position = jnp.concatenate([y * half + near, (1 - y) * half + near])
+    ok = position < length
+    valid = jnp.broadcast_to(ok[:, None], (rows, 128)).astype(F32)
+    sixty = jnp.arange(128) % 64
+    bias = jnp.where(ok, 0.0, -1e9)[:, None]
+    kaug = jnp.where(sixty == 0, bias, ((sixty > 0) & (sixty < 4)).astype(F32)).astype(BF16)
+    qs, ks, vs, ctx, aug, res, vec = attend(xs, wsquare, sf.reshape(32, 16, 128), kaug)
+    act, gres1, gwu, gwd, frows, fbias = feed(res, ct, valid, vec, wf)
+    gtok, dw, arows = retreat(gres1, xs, wsquare, qs, ks, vs, ctx, aug, kaug)
+    all_rows = jnp.concatenate([arows[0:2], frows[2:8]])
+    small = jnp.concatenate(
+        [
+            jnp.repeat(all_rows.reshape(8, 8, 128).transpose(1, 0, 2), 4, axis=0),
+            fbias[:, 0, :].reshape(32, 1, 128),
+            jnp.zeros((32, 7, 128), F32),
+        ],
+        axis=1,
+    ).astype(BF16)
+    six = (4, 2, 2, 2)
+    back = jnp.concatenate([act[half:], gtok[half:].astype(BF16)])
+    gu, gd, ga, gs, home = scatter(
+        [
+            gwu.reshape((4,) + six + (shard, width)),
+            gwd.reshape((4,) + six + (shard, width)),
+            dw.reshape((4,) + six + (shard, width)),
+        ],
+        small.reshape(six + (16, 128)),
+        back,
+        1,
+    )
+
+    def in_place(own, other):
+        mine = y == 0
+        first = jnp.where(mine, own, other)
+        second = jnp.where(mine, other, own)
+        return jnp.stack([first, second])[:, None]
+
+    activations = in_place(act[:half], home[:half])
+    grad_tokens = in_place(gtok[:half], home[half:].astype(F32))
+    grad_vectors = lax.dynamic_slice_in_dim(gs[0:8], (rank % 4) * 32, 32, axis=1)
+    return (
+        activations,
+        grad_tokens,
+        ga[0],
+        ga[1],
+        ga[2],
+        ga[3],
+        gu.transpose(1, 0, 2).reshape(shard, 4 * width),
+        gd.reshape(4 * shard, width),
+        grad_vectors,
+        gs[8],
+    )
+
+
 def solution(mesh):
     placed = (
         P(None, "dp", "seq", None),
@@ -267,8 +1153,9 @@
         P(("dp", "seq")),
         P(None, "dp", "seq", None),
     )
+    own = mesh.shape["dp"] == 16 and mesh.shape["seq"] == 2
     return jax.shard_map(
-        per_device,
+        paired if own else per_device,
         mesh=mesh,
         in_specs=placed,
         out_specs=(

time: 2270 us -> 603 us (0.27)
  waiting for transfers between devices: 1510 us -> 0 us
  Pallas kernels: 0 us -> 562 us
  matrix products: 414 us -> 0 us
  blocking collectives: 161 us -> 0 us
  other arithmetic: 108 us -> 9.69 us
  local copies, waits for them, and re-layouts: 53.1 us -> 18.9 us
    reduce_scatter x7 -> x0, waiting for transfers between devices: 825 us -> none  [the longest x1 361 us: per_device(): lax.psum_scatter(sums[4], ('dp', 'seq'), scatter_dimension=0, tiled=True)]
    pallas_call x0 -> x5, Pallas kernels: none -> 562 us  [the longest x1 169 us: gather(): pl.pallas_call(gather_kernel, out_shape=(jax.ShapeDtypeStruct((chunks, 4,...]
    unnamed x25 -> x0, waiting for transfers between devices: 428 us -> none
    dot_general x48 -> x0, matrix products: 414 us -> none  [the longest x2 46.5 us: per_device(): jnp.einsum('qhd,khd->hqk', grad_ctx_heads, val_heads, preferred_element_t...]
    all_gather x10 -> x0, waiting for transfers between devices: 252 us -> none  [the longest x1 67.1 us: fetch_forward(): lax.all_gather(w_down, ('dp', 'seq'), axis=0, tiled=True)]
    all_gather x2 -> x0, blocking collectives: 122 us -> none  [the longest x1 61.5 us: fetch_forward(): lax.all_gather(vectors, ('dp', 'seq'), axis=1, tiled=True)]
    convert_element_type x4 -> x3, other arithmetic: 59.2 us -> 1.57 us  [the longest x1 0.91 us: paired(): jnp.where(sixty == 0, bias, ((sixty > 0) & (sixty < 4)).astype(F32))]
    reduce_sum x11 -> x0, other arithmetic: 43.6 us -> none  [the longest x2 29.4 us: per_device(): jnp.sum(jnp.exp(scores - top), axis=-1, keepdims=True)]
  transfers between devices with their start and end apart: 21 -> 0, of which waited for: 14 -> 0; matrix products, arithmetic and copies ran while one was open for 20% -> 0% of each run, Pallas kernels for 0% -> 0%
where the time goes in v1:
time: 603 us; the launch traced here: 591 us
  Pallas kernels  562 us (93%)
  local copies, waits for them, and re-layouts  18.9 us (3%)
  other arithmetic  9.69 us (2%)
    pallas_call x1, Pallas kernels, gather(): pl.pallas_call(gather_kernel, out_shape=(jax.ShapeDtypeStruct((chunks, 4,...  169 us
    pallas_call x1, Pallas kernels, scatter(): pl.pallas_call(functools.partial(scatter_kernel, parts), out_shape=[jax.S...  153 us
    pallas_call x1, Pallas kernels, feed(): pl.pallas_call(feed_kernel, grid=(2 * chunks,), out_shape=(jax.ShapeDtype...  102 us
    pallas_call x1, Pallas kernels, retreat(): pl.pallas_call(retreat_kernel, out_shape=(jax.ShapeDtypeStruct((rows, wid...  80 us
    pallas_call x1, Pallas kernels, attend(): pl.pallas_call(attend_kernel, out_shape=(low, low, low, low, jax.ShapeDty...  57.3 us

profile of v1, /device:TPU:5, one launch (start us, length us, event | category | flops | bytes accessed | tf_op | source)
XLA Modules:
  0.0 591.3 jit_solution(16447349435193064162)
XLA Ops:
  0.6 0.0 copy-start
  0.7 0.0 copy-start.8
  0.7 0.6 copy-done
  1.3 0.6 constant_dynamic-slice_fusion.1
  1.9 0.1 pad.15.clone
  2.0 0.7 fusion.3
  2.7 0.7 tile.4
  3.4 0.1 tile.10
  3.5 1.3 maximum_maximum_fusion.1.sm
  4.8 0.9 select_convert_fusion.kaug
  5.7 1.0 broadcast_in_dim.59.valid
  6.7 0.8 bitcast_dynamic-update-slice_fusion.3
  7.5 0.8 bitcast_dynamic-update-slice_fusion.2
  8.4 0.8 bitcast_dynamic-update-slice_fusion.1
  9.2 0.8 bitcast_dynamic-update-slice_fusion
  10.1 1.0 fusion.2
  11.0 0.0 copy-done.8
  11.1 0.0 copy-start.6
  11.1 0.9 copy-done.6
  11.9 169.3 %gather.1 = (bf16[12,4,2,2,2,32,1024]{6,5,4,3,2,1,0:T(8,128)(2,1)}, bf16[4,2,2,2,16,128]{5,4,3,2,1,0:T(8,128)(2,1)}, bf16[2,512,1024]{2,1,0:T(8,128)(2,1)}, bf16[2,512,1024]{2,1,0:T(8,128)(2,1)}) custom-call(bf16[12,32,1024]{2,1,0:T(8,128)(2,1)} %copy-done.6, bf16[16,128]{1,0:T(8,128)(2,1)} %maximum_maximum_fusion.1.sm, bf16[2,1,512,1024]{3,2,1,0:T(8,128)(2,1)} %tok.1, ...), custom_call_target="tpu_custom_call" | custom-call | tf_op jit(solution)/shard_map/gather/pallas_call | solution.py:425
  181.2 57.3 %attend.1 = (bf16[1024,1024]{1,0:T(8,128)(2,1)}, bf16[1024,1024]{1,0:T(8,128)(2,1)}, bf16[1024,1024]{1,0:T(8,128)(2,1)}, bf16[1024,1024]{1,0:T(8,128)(2,1)}, bf1...) custom-call(bf16[1024,1024]{1,0:T(8,128)(2,1)} %bitcast.79, ...), custom_call_target="tpu_custom_call" | custom-call | flops 12884901888 | bytes 31457280 | tf_op jit(solution)/shard_map/attend/pallas_call | solution.py:735
  238.6 101.9 %feed.1 = (bf16[1024,1024]{1,0:T(8,128)(2,1)}, f32[1024,1024]{1,0:T(8,128)}, bf16[4,1024,1024]{2,1,0:T(8,128)(2,1)}, bf16[4,32,32,1024]{3,2,1,0:T(8,128)(2,1)}, f32[8,1024]{1,0:T(8,128)}, /*index=5*/f32[8,8,512]{2,1,0:T(8,128)}) custom-call(f32[1024,1024]{1,0:T(8,128)} %get-tuple-element.38.res, bf16[1024,1024]{1,0:T(8,128)(2,1)} %bitcast.81, ...), custom_call_target="tpu_custom_call" | custom-call | flops 51539607552 | bytes 83886080 | tf_op jit(solution)/shard_map/feed/pallas_call | solution.py:891
  340.4 0.0 copy-start.9
  340.4 80.0 %retreat.1 = (f32[1024,1024]{1,0:T(8,128)}, bf16[4,1024,1024]{2,1,0:T(8,128)(2,1)}, f32[8,1024]{1,0:T(8,128)}) custom-call(f32[1024,1024]{1,0:T(8,128)} %get-tuple-element.44.gres1, bf16[1024,1024]{1,0:T(8,128)(2,1)} %bitcast.80, bf16[12,1024,1024]{2,1,0:T(8,128)(2,1)} %bitcast.78, bf16[1024,1024]{1,0:T(8,128)(2,1)} %get-tuple-element.45.qs, ...), custom_call_target="tpu_custom_call" | custom-call | flops 30064771072 | bytes 41943040 | tf_op jit(solution)/shard_map/retreat/pallas_call | solution.py:1043
  420.5 0.0 copy-start.3
  420.5 0.9 slice.48
  421.4 0.0 copy-done.9
  421.4 0.9 slice.80
  422.4 0.8 maximum_maximum_fusion.refs_3_
  423.1 1.7 slice.79
  424.9 0.0 copy-done.3
  424.9 0.1 slice.51
  425.0 1.5 pad_maximum_fusion.refs_4_
  426.4 0.0 copy-start.2
  426.4 153.4 %scatter.1 = (f32[4,32,1024]{2,1,0:T(8,128)}, f32[4,32,1024]{2,1,0:T(8,128)}, f32[4,32,1024]{2,1,0:T(8,128)}, f32[16,128]{1,0:T(8,128)}, bf16[1024,1024]{1,0:T(8,128)(2,1)}) custom-call(bf16[4,4,2,2,2,32,1024]{6,5,4,3,2,1,0:T(8,128)(2,1)} %bitcast.64, bf16[4,4,2,2,2,32,1024]{6,5,4,3,2,1,0:T(8,128)(2,1)} %bitcast.65, ...), custom_call_target="tpu_custom_call" | custom-call | tf_op jit(solution)/shard_map/scatter/pallas_call | solution.py:626
  579.9 0.0 copy-start.5
  579.9 2.0 copy.28
  581.9 1.9 slice_bitcast_fusion
  583.8 0.0 copy-done.2
  583.8 0.0 copy-done.5
  583.8 0.0 copy-start.4
  583.8 0.6 fusion
  584.4 1.0 copy-done.4
  585.4 0.1 select_bitcast_fusion.1
  585.5 1.5 maximum_bitcast_fusion.1
  587.0 0.0 copy-start.10
  587.0 0.0 copy-start.7
  587.0 0.0 copy-start.1
  587.0 2.3 maximum_bitcast_fusion
  589.4 0.0 copy-done.10
  589.4 0.5 slice_bitcast_fusion.4
  589.9 0.7 constant_dynamic-slice_fusion
  590.5 0.0 copy-done.7
  590.5 0.8 copy.36
  591.3 0.0 copy-done.1
  (11 shorter events, 0.1 us)
Async XLA Ops:
  0.6 0.7 copy-start
  0.7 10.4 %copy-start.8 = (bf16[128,1024]{1,0:T(8,128)(2,1)S(1)}, bf16[128,1024]{1,0:T(8,128)(2,1)}, u32[]{:S(2)}) copy-start(bf16[128,1024]{1,0:T(8,128)(2,1)} %param.18) | copy-start | bytes 786436
  11.1 0.9 copy-start.6
  340.4 81.0 %copy-start.9 = (f32[8,1024]{1,0:T(8,128)S(1)}, f32[8,1024]{1,0:T(8,128)}, u32[]{:S(2)}) copy-start(f32[8,1024]{1,0:T(8,128)} %get-tuple-element.52) | copy-start | bytes 98308
  420.5 4.4 copy-start.3
  426.4 157.3 %copy-start.2 = (f32[1024,1024]{1,0:T(8,128)S(1)}, f32[1024,1024]{1,0:T(8,128)}, u32[]{:S(2)}) copy-start(f32[1024,1024]{1,0:T(8,128)} %get-tuple-element.54) | copy-start | bytes 12582916
  579.9 3.9 copy-start.5
  583.8 1.6 copy-start.4
  587.0 2.3 copy-start.10
  587.0 3.5 copy-start.7
  587.0 4.3 copy-start.1

commit v2 on v0

--- a/solution.py
+++ b/solution.py
@@ -1,8 +1,11 @@
+import functools
 import math
 
 import jax
 import jax.numpy as jnp
 from jax import lax
+from jax.experimental import pallas as pl
+from jax.experimental.pallas import tpu as pltpu
 from jax.sharding import PartitionSpec as P
 
 H = 16
@@ -253,6 +256,1062 @@
     )
 
 
+MESH = pl.DeviceIdType.MESH
+F32 = jnp.float32
+BF16 = jnp.bfloat16
+ANY = pl.ANY
+VMEM = pltpu.VMEM
+LOG2E = math.log2(math.e)
+LIMIT = 58 * 1024 * 1024
+GELU_C = math.sqrt(2.0 / math.pi)
+GELU_A = 0.044715
+
+
+def nt(a, b):
+    return lax.dot_general(a, b, (((1,), (1,)), ((), ())), preferred_element_type=F32)
+
+
+def nn(a, b):
+    return lax.dot_general(a, b, (((1,), (0,)), ((), ())), preferred_element_type=F32)
+
+
+def tn(a, b):
+    return lax.dot_general(a, b, (((0,), (0,)), ((), ())), preferred_element_type=F32)
+
+
+def place():
+    dp = lax.axis_index("dp")
+    return dp // 4, (dp // 2) % 2, dp % 2, lax.axis_index("seq")
+
+
+def device(z, x, c, y):
+    return (z * 4 + x * 2 + c, y)
+
+
+def greet(z, x, c, y):
+    barrier = pltpu.get_barrier_semaphore()
+    partners = [device(z, x, 1 - c, y), device(z, 1 - x, c, y), device(z, x, c, 1 - y)]
+    partners += [device((z + d) % 4, x, c, y) for d in (1, 2, 3)]
+    for partner in partners:
+        pl.semaphore_signal(barrier, inc=1, device_id=partner, device_id_type=MESH)
+    pl.semaphore_wait(barrier, len(partners))
+
+
+PHASES = 4
+SLOTS = 6
+
+
+def orders(half):
+    return ("yzxc", "zyxc" if half == 0 else "zxyc")
+
+
+def gather_copies(ref, rows, send, recv, order, phase, pos):
+    z, x, c, y = pos
+    every = slice(None)
+    done = order[:phase]
+    have = (
+        every if "z" in done else z,
+        every if "x" in done else x,
+        every if "c" in done else c,
+        every if "y" in done else y,
+        rows,
+    )
+
+    def copy(slot, target):
+        return pltpu.make_async_remote_copy(
+            src_ref=ref.at[have],
+            dst_ref=ref.at[have],
+            send_sem=send.at[slot],
+            recv_sem=recv.at[slot],
+            device_id=device(*target),
+            device_id_type=MESH,
+        )
+
+    axis = order[phase]
+    if axis == "z":
+        return [copy(2 + d, ((z + d) % 4, x, c, y)) for d in (1, 2, 3)]
+    if axis == "x":
+        return [copy(0, (z, 1 - x, c, y))]
+    if axis == "y":
+        return [copy(1, (z, x, c, 1 - y))]
+    return [copy(2, (z, x, 1 - c, y))]
+
+
+def gather_phase(ref, rows, send, recv, phase, pos, half):
+    for core in (0, 1):
+        for odd in (0, 1):
+            if core == 0 and odd == 1:
+                continue
+            order = orders(odd)[core]
+            here = pos[2] == core
+            if core == 1:
+                here = here & (half == odd)
+
+            @pl.when(here)
+            def _():
+                if phase > 0:
+                    for copy in gather_copies(ref, rows, send, recv, order, phase - 1, pos):
+                        copy.wait_recv()
+                if phase < PHASES:
+                    for copy in gather_copies(ref, rows, send, recv, order, phase, pos):
+                        copy.start()
+
+
+def gather_sent(ref, rows, send, recv, pos, half):
+    for core in (0, 1):
+        for odd in (0, 1):
+            if core == 0 and odd == 1:
+                continue
+            order = orders(odd)[core]
+            here = pos[2] == core
+            if core == 1:
+                here = here & (half == odd)
+
+            @pl.when(here)
+            def _():
+                for phase in range(PHASES):
+                    for copy in gather_copies(ref, rows, send, recv, order, phase, pos):
+                        copy.wait_send()
+
+
+def lanes(shape):
+    return lax.broadcasted_iota(jnp.int32, shape, len(shape) - 1)
+
+
+def norm(v):
+    center = v - jnp.mean(v, axis=-1, keepdims=True)
+    inverse = lax.rsqrt(jnp.mean(center * center, axis=-1, keepdims=True) + EPSILON)
+    return center * inverse, inverse
+
+
+def norm_back(g, normed, inverse, gain):
+    gn = g * gain
+    inner = gn - jnp.mean(gn, axis=-1, keepdims=True) - normed * jnp.mean(gn * normed, axis=-1, keepdims=True)
+    return inner * inverse
+
+
+def rowsum(v):
+    return jnp.sum(v, axis=0, keepdims=True)
+
+
+def blocks(rows, block, body):
+    def run(b, carry):
+        body(pl.ds(pl.multiple_of(b * block, block), block))
+        return carry
+
+    lax.fori_loop(0, rows // block, run, 0)
+
+
+def tiles(width, tile, body):
+    def run(b, carry):
+        body(b, pl.ds(pl.multiple_of(b * tile, tile), tile))
+        return carry
+
+    lax.fori_loop(0, width // tile, run, 0)
+
+
+def forward_kernel(
+    wq, wk, wv, wo, wup, wdown, sm, tok, cot, kaug, valid,
+    wfa, wfd, sf, xs_o, q_o, k_o, v_o, ctx_o, aug_o, res_o, low_o, act_o, slope_o, back_o, gdn_o, out_o, vec, rows_out,
+    xs, ct, qs, ks, vs, ctx, aug, res, acc, low, actv, slope, wbuf, dbuf, small,
+    send, recv, place_sem, own_sem, swap_send, swap_recv, wsem, dsem, out_sem,
+):
+    pos = place()
+    z, x, c, y = pos
+    rows, width = xs.shape
+    half = rows // 2
+    chunks = 24
+    high = 16
+
+    first = [pltpu.make_async_copy(w, wfa.at[i, z, x, c, y], place_sem.at[i]) for i, w in enumerate((wq, wk, wv, wo))]
+    for j in range(4):
+        first.append(
+            pltpu.make_async_copy(
+                wup.at[:, width * j : width * (j + 1)], wfa.at[4 + j, z, x, c, y], place_sem.at[4 + j]
+            )
+        )
+    for j in range(4):
+        first.append(
+            pltpu.make_async_copy(wdown.at[:, 256 * j : 256 * (j + 1)], wfd.at[j, z, x, c, y], place_sem.at[8 + j])
+        )
+    first.append(pltpu.make_async_copy(sm, sf.at[z, x, c, y], place_sem.at[12]))
+    for copy in first:
+        copy.start()
+    mine = [
+        pltpu.make_async_copy(tok.at[y, 0], xs.at[pl.ds(0, half)], own_sem.at[0]),
+        pltpu.make_async_copy(cot.at[y, 0], ct.at[pl.ds(0, half)], own_sem.at[1]),
+    ]
+    for copy in mine:
+        copy.start()
+    greet(*pos)
+    for copy in first:
+        copy.wait()
+
+    piece = half // 8
+
+    def swap(src, dst, slot, index):
+        at = pl.multiple_of(index * piece, piece)
+        return pltpu.make_async_remote_copy(
+            src_ref=src.at[1 - y, 0, pl.ds(at, piece)],
+            dst_ref=dst.at[pl.ds(half + at, piece)],
+            send_sem=swap_send.at[slot, index],
+            recv_sem=swap_recv.at[slot, index],
+            device_id=device(z, x, c, 1 - y),
+            device_id_type=MESH,
+        )
+
+    def chunk(index, kind):
+        odd = index % 2
+        if kind == 0:
+            return (wfa.at[index // 2], pl.ds(pl.multiple_of(odd * 16, 16), 16), send.at[index], recv.at[index])
+        return (wfd.at[index // 2 - 8], pl.ds(pl.multiple_of(odd * 64, 64), 64), send.at[index], recv.at[index])
+
+    tiny = (sf, slice(None), send.at[chunks], recv.at[chunks])
+
+    def step(t, carry):
+        for phase in range(PHASES + 1):
+            index = t - phase
+
+            @pl.when((index >= 0) & (index < high))
+            def _():
+                gather_phase(*chunk(index, 0), phase, pos, index % 2)
+
+            @pl.when((index >= high) & (index < chunks))
+            def _():
+                gather_phase(*chunk(index, 1), phase, pos, index % 2)
+
+            @pl.when(index == 0)
+            def _():
+                gather_phase(*tiny, phase, pos, 0)
+
+        @pl.when(t < 4)
+        def _():
+            swap(tok, xs, 0, 2 * t).start()
+            swap(tok, xs, 0, 2 * t + 1).start()
+
+        @pl.when((t >= 12) & (t < 20))
+        def _():
+            swap(cot, ct, 1, t - 12).start()
+
+        return carry
+
+    def advance(start, stop):
+        lax.fori_loop(start, stop, step, 0)
+
+    def weight(index, slot):
+        return pltpu.make_async_copy(wfa.at[index], wbuf.at[slot], wsem.at[slot])
+
+    def square(slot, cols):
+        return wbuf[slot, :, :, :, :, :, cols].reshape(width, cols.size)
+
+    def save(src, dst, slot):
+        copy = pltpu.make_async_copy(src, dst, out_sem.at[slot])
+        copy.start()
+        return copy
+
+    advance(0, 6)
+    weight(0, 0).start()
+    for index in range(8):
+        swap(tok, xs, 0, index).wait_recv()
+    for copy in mine:
+        copy.wait()
+    saves = [save(xs, xs_o, 0)]
+    gathered = pltpu.make_async_copy(sf, small, own_sem.at[2])
+    gathered.start()
+    gathered.wait()
+    tiles32 = [small[a, b, d, e].astype(F32) for a in range(4) for b in range(2) for d in range(2) for e in range(2)]
+    for g in range(8):
+        vec[0:8, 128 * g : 128 * g + 128] = sum(tiles32[4 * g + s] for s in range(4))[0:8]
+    for r in range(4):
+        for g in range(8):
+            vec[8 + r : 9 + r, 128 * g : 128 * g + 128] = tiles32[8 * r + g][8:9]
+    vec[12:16, :] = jnp.zeros((4, width), F32)
+
+    for i, dst in enumerate((qs, ks, vs)):
+        if i > 0:
+            advance(4 + 2 * i, 6 + 2 * i)
+            weight(i, i % 2).start()
+        weight(i, i % 2).wait()
+
+        def project(n, cols):
+            out = nn(xs[...], square(i % 2, cols))
+            if i == 0:
+                out = (out + vec[0:1, cols]) * (LOG2E / 8.0)
+            elif i == 2:
+                out = out + vec[1:2, cols]
+            dst[:, cols] = out.astype(BF16)
+
+        tiles(width, 256, project)
+        saves.append(save(dst, (q_o, k_o, v_o)[i], 1 + i))
+    advance(10, 12)
+    weight(3, 1).start()
+
+    block = 256
+    low1 = (lanes((1, 128)) < 64).astype(F32).astype(BF16)
+    high1 = (lanes((1, 128)) >= 64).astype(F32).astype(BF16)
+    ones1 = (lanes((1, 128)) % 64 == 0).astype(F32).astype(BF16)
+    qlane = lanes((block, 128))
+    sixty = qlane % 64
+
+    def pair(hp, carry):
+        cols = pl.ds(pl.multiple_of(hp * 128, 128), 128)
+        k2 = ks[:, cols]
+        v2 = vs[:, cols]
+        ka = k2 * low1 + kaug[...] * high1
+        kb = k2 * high1 + kaug[...] * low1
+
+        def query_block(sl):
+            q2 = qs[sl, cols]
+            parts = []
+            for own, other, kk in ((low1, high1, ka), (high1, low1, kb)):
+                s = nt(q2 * own + ones1 * other, kk)
+                top = jnp.max(s, axis=1, keepdims=True)
+                e = jnp.exp2(s - top)
+                total = jnp.sum(e, axis=1, keepdims=True)
+                o = nn(e.astype(BF16), v2)
+                parts.append((o / total, -(top + jnp.log2(total))))
+            lower = qlane < 64
+            ctx[sl, cols] = jnp.where(lower, parts[0][0], parts[1][0]).astype(BF16)
+            neg = jnp.where(lower, parts[1][1], parts[0][1])
+            hi = neg.astype(BF16).astype(F32)
+            mid = (neg - hi).astype(BF16).astype(F32)
+            lo = neg - hi - mid
+            aug[sl, cols] = jnp.where(
+                sixty == 0,
+                1.0,
+                jnp.where(sixty == 1, hi, jnp.where(sixty == 2, mid, jnp.where(sixty == 3, lo, 0.0))),
+            ).astype(BF16)
+
+        blocks(rows, block, query_block)
+        advance(12 + (hp * 3) // 2, 12 + ((hp + 1) * 3) // 2)
+        return carry
+
+    lax.fori_loop(0, width // 128, pair, 0)
+    saves.append(save(ctx, ctx_o, 4))
+    saves.append(save(aug, aug_o, 5))
+    weight(3, 1).wait()
+    weight(4, 0).start()
+
+    def project_out(n, cols):
+        out = nn(ctx[...], square(1, cols))
+        res[:, cols] = xs[:, cols].astype(F32) + (out + vec[2:3, cols])
+
+    tiles(width, 256, project_out)
+    weight(5, 1).start()
+    saves.append(save(res, res_o, 6))
+
+    def normalize(sl):
+        normed, _ = norm(res[sl, :])
+        low[sl, :] = (normed * vec[3:4, :] + vec[4:5, :]).astype(BF16)
+
+    blocks(rows, block, normalize)
+    saves.append(save(low, low_o, 7))
+
+    for j in range(4):
+        weight(4 + j, j % 2).wait()
+
+        def climb(n, cols):
+            up = nn(low[...], square(j % 2, cols)) + vec[8 + j : 9 + j, cols]
+            sq = up * up
+            t = jnp.tanh(up * (GELU_C + (GELU_C * GELU_A) * sq))
+            hf = 0.5 * up
+            actv[j, :, cols] = (hf + hf * t).astype(BF16)
+            slope[j, :, cols] = (
+                0.5 + 0.5 * t + hf * (1.0 - t * t) * (GELU_C + (3.0 * GELU_C * GELU_A) * sq)
+            ).astype(BF16)
+
+        tiles(width, 256, climb)
+        if j < 2:
+            weight(6 + j, j).start()
+        saves.append(save(actv.at[j], act_o.at[j], 8 + j))
+        saves.append(save(slope.at[j], slope_o.at[j], 12 + j))
+        advance(24 + j, 25 + j)
+
+    def shaft(j, slot):
+        return pltpu.make_async_copy(wfd.at[j], dbuf.at[slot], dsem.at[slot])
+
+    shaft(0, 0).start()
+    shaft(1, 1).start()
+    for j in range(4):
+        shaft(j, j % 2).wait()
+        cols = slice(256 * j, 256 * (j + 1))
+        total = vec[5:6, cols]
+        for k in range(4):
+            total = total + nn(actv[k], dbuf[j % 2, k].reshape(width, 256))
+        acc[:, cols] = total
+        if j < 2:
+            shaft(2 + j, j).start()
+
+    for index in range(8):
+        swap(cot, ct, 1, index).wait_recv()
+    saves[1].wait()
+    rows_out[...] = jnp.zeros_like(rows_out)
+
+    def middle(sl):
+        normed, _ = norm(res[sl, :])
+        hidden = normed * vec[3:4, :] + vec[4:5, :]
+        normed, inverse = norm(hidden + acc[sl, :])
+        ok = valid[sl, 0:1]
+        qs[sl, :] = ((normed * vec[6:7, :] + vec[7:8, :]) * ok).astype(BF16)
+        g = ct[sl, :].astype(F32) * ok
+        back = norm_back(g, normed, inverse, vec[6:7, :])
+        acc[sl, :] = back
+        gd = back.astype(BF16)
+        ct[sl, :] = gd
+        rows_out[6:7, :] += rowsum(g * normed)
+        rows_out[7:8, :] += rowsum(g)
+        rows_out[5:6, :] += rowsum(gd.astype(F32))
+
+    blocks(rows, block, middle)
+    saves.append(save(qs, out_o, 16))
+    saves.append(save(acc, back_o, 17))
+    saves.append(save(ct, gdn_o, 18))
+
+    def finish(index, carry):
+        @pl.when(index < high)
+        def _():
+            gather_sent(*chunk(index, 0), pos, index % 2)
+
+        @pl.when(index >= high)
+        def _():
+            gather_sent(*chunk(index, 1), pos, index % 2)
+
+        return carry
+
+    lax.fori_loop(0, chunks, finish, 0)
+    gather_sent(*tiny, pos, 0)
+    for slot, (src, dst) in enumerate(((tok, xs), (cot, ct))):
+        for index in range(8):
+            swap(src, dst, slot, index).wait_send()
+    for k, copy in enumerate(saves):
+        if k != 1:
+            copy.wait()
+
+
+def forward_pass(weights, sm, tok, cot, kaug, valid):
+    width = tok.shape[3]
+    rows = 2 * tok.shape[2]
+    low = jax.ShapeDtypeStruct((rows, width), BF16)
+    full = jax.ShapeDtypeStruct((rows, width), F32)
+    wide = jax.ShapeDtypeStruct((4, rows, width), BF16)
+    six = (4, 2, 2, 2)
+    vmem = pl.BlockSpec(memory_space=VMEM)
+    hbm = pl.BlockSpec(memory_space=ANY)
+    dma = pltpu.SemaphoreType.DMA
+    return pl.pallas_call(
+        forward_kernel,
+        out_shape=(
+            jax.ShapeDtypeStruct((8,) + six + (32, width), BF16),
+            jax.ShapeDtypeStruct((4,) + six + (128, 256), BF16),
+            jax.ShapeDtypeStruct(six + (16, 128), BF16),
+            low, low, low, low, low, low, full, low, wide, wide, full, low, low,
+            jax.ShapeDtypeStruct((16, width), F32),
+            jax.ShapeDtypeStruct((8, width), F32),
+        ),
+        in_specs=[vmem] * 7 + [hbm] * 2 + [vmem] * 2,
+        out_specs=[hbm] * 16 + [vmem] * 2,
+        scratch_shapes=[VMEM((rows, width), BF16)] * 7
+        + [
+            VMEM((rows, width), F32),
+            VMEM((rows, width), F32),
+            VMEM((rows, width), BF16),
+            VMEM((4, rows, width), BF16),
+            VMEM((4, rows, width), BF16),
+            VMEM((2,) + six + (32, width), BF16),
+            VMEM((2,) + six + (128, 256), BF16),
+            VMEM(six + (16, 128), BF16),
+            dma((25, SLOTS)),
+            dma((25, SLOTS)),
+            dma((13,)),
+            dma((3,)),
+            dma((2, 8)),
+            dma((2, 8)),
+            dma((2,)),
+            dma((2,)),
+            dma((19,)),
+        ],
+        compiler_params=pltpu.CompilerParams(collective_id=0, has_side_effects=True, vmem_limit_bytes=LIMIT),
+        cost_estimate=pl.CostEstimate(flops=2 * 14 * rows * width * width, bytes_accessed=90 << 20, transcendentals=1 << 24),
+        name="forward_pass",
+    )(*weights, sm, tok, cot, kaug, valid)
+
+
+CHUNKS = 12
+DEPTH = 4
+STARTS = (0, 1, 2, 3, 4, 5, 6, 7, 8, 12, 16, 17)
+TICKS = STARTS[-1] + PHASES + 1
+
+
+def chunk_at(tick):
+    index = jnp.where(tick <= 8, tick, jnp.where(tick <= 12, 9, tick - 6))
+    return index, (tick >= 0) & ((tick <= 8) | (tick == 12) | ((tick >= 16) & (tick <= 17)))
+
+
+MODES = 3
+
+
+def mode_of(core, index):
+    return jnp.where(core == 0, 0, jnp.where(index < 9, 1, 2))
+
+
+def scatter_copies(mode, phase, grad, bufs, send, recv, pos):
+    z, x, c, y = pos
+    b0, b1, b2, b3 = bufs
+
+    def remote(src, dst, slot, target):
+        return pltpu.make_async_remote_copy(
+            src_ref=src,
+            dst_ref=dst,
+            send_sem=send.at[slot],
+            recv_sem=recv.at[slot],
+            device_id=device(*target),
+            device_id_type=MESH,
+        )
+
+    across = (z, 1 - x, c, y)
+    beside = (z, x, c, 1 - y)
+    if phase == 0:
+        return [remote(grad.at[:, :, 1 - c], b0, 2, (z, x, 1 - c, y))]
+    if phase == 1:
+        if mode == 1:
+            return [remote(b0.at[:, :, 1 - y], b1, 1, beside)]
+        return [remote(b0.at[:, 1 - x], b1, 0, across)]
+    if phase == 2:
+        if mode == 0:
+            return [
+                remote(b1.at[(z + d) % 4], b2.at[pl.ds(2 * (d - 1), 2)], 2 + d, ((z + d) % 4, x, c, y))
+                for d in (1, 2, 3)
+            ]
+        if mode == 1:
+            return [remote(b1.at[:, 1 - x], b2.at[pl.ds(0, 4)], 0, across)]
+        return [remote(b1.at[:, 1 - y], b2.at[pl.ds(0, 4)], 1, beside)]
+    if mode == 0:
+        return [remote(b1.at[z, 1 - y], b3.at[0], 1, beside)]
+    return [remote(b2.at[(z + d) % 4], b3.at[d - 1], 2 + d, ((z + d) % 4, x, c, y)) for d in (1, 2, 3)]
+
+
+def scatter_add(mode, phase, own, bufs, out, pos):
+    z, x, c, y = pos
+    b0, b1, b2, b3 = bufs
+
+    def plus(dst, a, b):
+        dst[...] = (a.astype(F32) + b.astype(F32)).astype(dst.dtype)
+
+    def each(body):
+        def run(zz, carry):
+            body(zz)
+            return carry
+
+        lax.fori_loop(0, 4, run, 0)
+
+    if phase == 0:
+
+        def body(zz):
+            plus(b0.at[zz], own[zz], b0[zz])
+
+        each(body)
+    elif phase == 1:
+
+        def body(zz):
+            plus(b1.at[zz], b0[zz, :, y] if mode == 1 else b0[zz, x], b1[zz])
+
+        each(body)
+    elif mode == 0:
+        if phase == 2:
+            total = b1[z].astype(F32)
+            for d in range(3):
+                total = total + b2[pl.ds(2 * d, 2)].astype(F32)
+            b1[z] = total.astype(BF16)
+        else:
+            out[...] = b1[z, y].astype(F32) + b3[0].astype(F32)
+    elif phase == 2:
+
+        def body(zz):
+            plus(b2.at[zz], b1[zz, x] if mode == 1 else b1[zz, y], b2[zz])
+
+        each(body)
+    else:
+        total = b2[z].astype(F32)
+        for d in range(3):
+            total = total + b3[d].astype(F32)
+        out[...] = total
+
+
+def scatter_phase(phase, mode, grad, own, own_sem, bufs, out, send, recv, credit, index, pos):
+    z, x, c, y = pos
+
+    def mine():
+        return pltpu.make_async_copy(grad.at[:, :, c], own, own_sem)
+
+    if phase == 0:
+        mine().start()
+        if credit is not None:
+
+            @pl.when(index >= DEPTH)
+            def _():
+                pl.semaphore_wait(credit, 1)
+
+    if phase == 1:
+        mine().wait()
+    for which in range(MODES):
+
+        @pl.when(mode == which)
+        def _():
+            if phase > 0:
+                for copy in scatter_copies(which, phase - 1, grad, bufs, send, recv, pos):
+                    copy.wait_recv()
+                if phase == 2:
+                    for copy in scatter_copies(which, 1, grad, bufs, send, recv, pos):
+                        copy.wait_send()
+                scatter_add(which, phase - 1, own, bufs, out, pos)
+            if phase < PHASES:
+                for copy in scatter_copies(which, phase, grad, bufs, send, recv, pos):
+                    copy.start()
+
+    if phase == 2 and credit is not None:
+
+        @pl.when(index < CHUNKS - DEPTH)
+        def _():
+            pl.semaphore_signal(credit, inc=1, device_id=device(z, x, 1 - c, y), device_id_type=MESH)
+
+
+def scatter_sent(mode, grad, bufs, send, recv, pos):
+    for which in range(MODES):
+
+        @pl.when(mode == which)
+        def _():
+            for phase in (0, 2, 3):
+                for copy in scatter_copies(which, phase, grad, bufs, send, recv, pos):
+                    copy.wait_send()
+
+
+def backward_kernel(
+    wfa, wfd, xs_i, q_i, k_i, v_i, ctx_i, aug_i, res_i, low_i, act_i, slope_i, back_i, gdn_i, out_i, vec, rows_in, kaug,
+    gw, act_o, gtok_o, outs, small_out,
+    acc, rbuf, gdn, low, quad, duo, wbuf, dbuf, stage, own, b0, b1, b2, b3, home, rows_sum, bias_sum,
+    small_g, small_own, s0, s1, s2, s3,
+    send, recv, own_sem, credit, swap_send, swap_recv, load_sem, rsem, wsem, dsem, stage_sem, out_sem,
+):
+    pos = place()
+    z, x, c, y = pos
+    rows, width = acc.shape
+    half = rows // 2
+    block = 256
+
+    def load(src, dst, slot):
+        return pltpu.make_async_copy(src, dst, load_sem.at[slot])
+
+    loads = [load(act_i.at[k], quad.at[k], k) for k in range(4)]
+    loads += [load(gdn_i, gdn, 4), load(low_i, low, 5), load(back_i, acc, 6)]
+    loads += [load(out_i.at[pl.ds(0, half)], duo.at[1, pl.ds(0, half)], 7), load(slope_i.at[0], duo.at[0], 8)]
+    for k in (4, 0, 1, 2, 3, 5, 6, 7, 8):
+        loads[k].start()
+    greet(*pos)
+
+    away = pltpu.make_async_remote_copy(
+        src_ref=out_i.at[pl.ds(half, half)],
+        dst_ref=act_o.at[y, 0],
+        send_sem=swap_send.at[0],
+        recv_sem=swap_recv.at[0],
+        device_id=device(z, x, c, 1 - y),
+        device_id_type=MESH,
+    )
+    away.start()
+
+    def views(index):
+        slot = index % DEPTH
+        return (b0.at[slot], b1.at[index], b2.at[index], b3.at[index])
+
+    small_bufs = (s0, s1, s2, s3)
+
+    def step(t, carry):
+        for phase in range(PHASES + 1):
+            index, there = chunk_at(t - phase)
+
+            @pl.when(there)
+            def _():
+                scatter_phase(
+                    phase, mode_of(c, index), gw.at[index], own.at[index % 2], own_sem.at[index % 2], views(index),
+                    outs.at[index], send.at[index], recv.at[index], credit, index, pos,
+                )
+
+            @pl.when(t - phase == STARTS[-1])
+            def _():
+                scatter_phase(
+                    phase, mode_of(c, 0), small_g, small_own, own_sem.at[2], small_bufs, small_out,
+                    send.at[CHUNKS], recv.at[CHUNKS], None, 0, pos,
+                )
+
+        return carry
+
+    def advance(start, stop):
+        lax.fori_loop(start, stop, step, 0)
+
+    def weight(index, slot):
+        return pltpu.make_async_copy(wfa.at[index], wbuf.at[slot], wsem.at[slot])
+
+    def shaft(j, slot):
+        return pltpu.make_async_copy(wfd.at[:, j], dbuf.at[slot], dsem.at[slot])
+
+    def store(index, slot):
+        return pltpu.make_async_copy(stage.at[slot], gw.at[index], stage_sem.at[slot])
+
+    weight(4, 0).start()
+    shaft(0, 0).start()
+    rows_sum[...] = rows_in[...]
+    bias_sum[...] = jnp.zeros_like(bias_sum)
+
+    for k in (4, 0, 1, 2, 3):
+        loads[k].wait()
+    for jj in range(4):
+        slot = jj % 2
+        if jj >= 2:
+            store(jj - 2, slot).wait()
+
+        def quarter(k, carry):
+            part = tn(quad[k], gdn[:, 256 * jj : 256 * (jj + 1)]).astype(BF16).reshape(2, 2, 2, 4, 32, 256)
+            for q in range(4):
+                stage[slot, k, :, :, :, :, 256 * q : 256 * (q + 1)] = part[:, :, :, q]
+            return carry
+
+        lax.fori_loop(0, 4, quarter, 0)
+        store(jj, slot).start()
+        if jj >= 2:
+            advance(jj - 2, jj - 1)
+    loads[5].wait()
+    loads[6].wait()
+    loads[7].wait()
+    keep = pltpu.make_async_copy(duo.at[1, pl.ds(0, half)], act_o.at[y, 0], out_sem.at[0])
+    keep.start()
+    for k, src in enumerate((q_i, k_i, v_i, ctx_i)):
+        load(src, quad.at[k], k).start()
+    small_block = 128
+    load(res_i.at[pl.ds(0, small_block)], rbuf.at[0], 9).start()
+
+    def slope_load(j):
+        return load(slope_i.at[j], duo.at[j % 2], 8 - j % 2)
+
+    def square_rows(slot, n):
+        return wbuf[slot, n].reshape(256, width)
+
+    for j in range(4):
+        slot = j % 2
+        slope_load(j).wait()
+        shaft(j, slot).wait()
+        if j == 0:
+            keep.wait()
+        if j < 3:
+            slope_load(j + 1).start()
+            weight(5 + j, 1 - slot).start()
+            shaft(j + 1, 1 - slot).start()
+        for n in range(4):
+            cols = slice(256 * n, 256 * (n + 1))
+            total = nt(gdn[:, 0:256], dbuf[slot, 0, n // 2, n % 2].reshape(256, 256))
+            for jj in range(1, 4):
+                total = total + nt(
+                    gdn[:, 256 * jj : 256 * (jj + 1)], dbuf[slot, jj, n // 2, n % 2].reshape(256, 256)
+                )
+            gu = (duo[slot, :, cols].astype(F32) * total).astype(BF16)
+            duo[slot, :, cols] = gu
+            bias_sum[8 * j : 8 * j + 1, cols] = rowsum(gu.astype(F32))
+        store(2 + j, slot).wait()
+        advance(2 + j, 3 + j)
+
+        def up_grad(n, cols):
+            part = tn(low[...], duo[slot, :, cols]).astype(BF16)
+            stage[slot, :, :, :, :, :, cols] = part.reshape(4, 2, 2, 2, 32, 256)
+
+        tiles(width, 256, up_grad)
+        store(4 + j, slot).start()
+        weight(4 + j, slot).wait()
+        for n in range(4):
+            cols = slice(256 * n, 256 * (n + 1))
+            acc[:, cols] += nt(duo[slot], square_rows(slot, n))
+    weight(3, 0).start()
+    load(xs_i, duo.at[0], 8).start()
+    load(aug_i, duo.at[1], 7).start()
+
+    for b in range(rows // small_block):
+        sl = slice(b * small_block, (b + 1) * small_block)
+        load(res_i.at[pl.ds(b * small_block, small_block)], rbuf.at[b % 2], 9 + b % 2).wait()
+        if b + 1 < rows // small_block:
+            load(res_i.at[pl.ds((b + 1) * small_block, small_block)], rbuf.at[(b + 1) % 2], 9 + (b + 1) % 2).start()
+        normed, inverse = norm(rbuf[b % 2])
+        g = acc[sl, :]
+        back = norm_back(g, normed, inverse, vec[3:4, :])
+        acc[sl, :] = back
+        gat = back.astype(BF16)
+        gdn[sl, :] = gat
+        rows_sum[3:4, :] += rowsum(g * normed)
+        rows_sum[4:5, :] += rowsum(g)
+        rows_sum[2:3, :] += rowsum(gat.astype(F32))
+
+    store(6, 0).wait()
+    advance(6, 7)
+    for k in range(4):
+        load((q_i, k_i, v_i, ctx_i)[k], quad.at[k], k).wait()
+
+    def out_grad(n, cols):
+        part = tn(quad[3], gdn[:, cols]).astype(BF16)
+        stage[0, :, :, :, :, :, cols] = part.reshape(4, 2, 2, 2, 32, 256)
+
+    tiles(width, 256, out_grad)
+    store(8, 0).start()
+    weight(3, 0).wait()
+    for n in range(4):
+        low[:, 256 * n : 256 * (n + 1)] = nt(gdn[...], square_rows(0, n)).astype(BF16)
+    store(7, 1).wait()
+    advance(7, 8)
+    weight(0, 0).start()
+    load(xs_i, duo.at[0], 8).wait()
+    load(aug_i, duo.at[1], 7).wait()
+    store(8, 0).wait()
+
+    qs, ks, vs, ctx = (quad.at[k] for k in range(4))
+    xs, aug = duo.at[0], duo.at[1]
+    low1 = (lanes((1, 128)) < 64).astype(F32).astype(BF16)
+    high1 = (lanes((1, 128)) >= 64).astype(F32).astype(BF16)
+    ones1 = (lanes((1, 128)) % 64 < 2).astype(F32).astype(BF16)
+    alane = lanes((rows, 128))
+    lower = alane < 64
+    sixty = alane % 64
+
+    def token_grad(k, first, slot, target):
+        def run(n, carry):
+            src = pl.ds(pl.multiple_of(first + n * 256, 256), 256)
+            dst = pl.ds(pl.multiple_of(target + n * 256, 256), 256)
+            part = tn(xs[...], quad[k, :, src]).astype(BF16)
+            stage[slot, :, :, :, :, :, dst] = part.reshape(4, 2, 2, 2, 32, 256)
+            return carry
+
+        lax.fori_loop(0, 2, run, 0)
+
+    def pair(hp, carry):
+        @pl.when(hp == 4)
+        def _():
+            token_grad(0, 0, 0, 0)
+            token_grad(1, 0, 0, 512)
+            store(9, 0).start()
+            token_grad(2, 0, 1, 0)
+            store(9, 0).wait()
+
+        advance(8 + hp, 9 + hp)
+        cols = pl.ds(pl.multiple_of(hp * 128, 128), 128)
+        q2 = qs[:, cols]
+        g2 = low[:, cols]
+        au = aug[:, cols]
+        prod = g2.astype(F32) * ctx[:, cols].astype(F32)
+        da = -jnp.sum(jnp.where(lower, prod, 0.0), axis=1, keepdims=True)
+        db = -jnp.sum(jnp.where(lower, 0.0, prod), axis=1, keepdims=True)
+        neg = jnp.where(lower, db, da)
+        hi = neg.astype(BF16).astype(F32)
+        daug = jnp.where(sixty == 0, hi, jnp.where(sixty == 1, neg - hi, 0.0)).astype(BF16)
+        qa = (q2 * low1 + au * high1, q2 * high1 + au * low1)
+        ga = (g2 * low1 + daug * high1, g2 * high1 + daug * low1)
+        gq = []
+        gk_all = []
+        gv_all = []
+        for head in range(2):
+            mine, other = (low1, high1) if head == 0 else (high1, low1)
+            total = jnp.zeros((128, rows), F32)
+            gks = []
+            gvs = []
+            for b in range(rows // block):
+                sl = slice(b * block, (b + 1) * block)
+                k2 = ks[sl, cols]
+                v2 = vs[sl, cols]
+                s = nt(k2 * mine + kaug[sl, :] * other, qa[head])
+                p = jnp.exp2(s)
+                gp = nt(v2 * mine + ones1 * other, ga[head])
+                ds = (p * gp).astype(BF16)
+                gvs.append(nn(p.astype(BF16), g2).astype(BF16) * mine)
+                gks.append((nn(ds, q2) * (1.0 / LOG2E)).astype(BF16) * mine)
+                total = total + tn(k2, ds)
+            gq.append(total)
+            gk_all.append(gks)
+            gv_all.append(gvs)
+        for b in range(rows // block):
+            sl = slice(b * block, (b + 1) * block)
+            ks[sl, cols] = gk_all[0][b] + gk_all[1][b]
+            vs[sl, cols] = gv_all[0][b] + gv_all[1][b]
+        both = jnp.concatenate([gq[0][0:64], gq[1][64:128]], axis=0) * 0.125
+        qs[:, cols] = both.T.astype(BF16)
+        return carry
+
+    weight(1, 1).start()
+    lax.fori_loop(0, 8, pair, 0)
+    token_grad(0, 512, 1, 512)
+    store(10, 1).start()
+    token_grad(1, 512, 0, 0)
+    token_grad(2, 512, 0, 512)
+    store(11, 0).start()
+
+    def bias_rows(n, cols):
+        rows_sum[0:1, cols] = rowsum(quad[0, :, cols].astype(F32))
+        rows_sum[1:2, cols] = rowsum(quad[2, :, cols].astype(F32))
+
+    tiles(width, 256, bias_rows)
+    for zz in range(4):
+        for s in range(8):
+            g = 2 * zz + s // 4
+            tile = jnp.concatenate(
+                [
+                    rows_sum[:, 128 * g : 128 * (g + 1)],
+                    bias_sum[8 * zz : 8 * zz + 8, 128 * s : 128 * (s + 1)],
+                ],
+                axis=0,
+            )
+            small_g[zz, s // 4, (s // 2) % 2, s % 2] = tile.astype(BF16)
+    store(10, 1).wait()
+    advance(16, 17)
+    store(11, 0).wait()
+    advance(17, 18)
+
+    def token_rows(k, slot, sl):
+        for n in range(4):
+            cols = slice(256 * n, 256 * (n + 1))
+            acc[sl, cols] += nt(quad[k, sl], square_rows(slot, n))
+
+    weight(0, 0).wait()
+    token_rows(0, 0, slice(0, rows))
+    weight(2, 0).start()
+    weight(1, 1).wait()
+    token_rows(1, 1, slice(0, rows))
+    weight(2, 0).wait()
+    token_rows(2, 0, slice(half, rows))
+    low[0:half, :] = acc[half:rows, :].astype(BF16)
+    turn = pltpu.make_async_remote_copy(
+        src_ref=low.at[pl.ds(0, half)],
+        dst_ref=home,
+        send_sem=swap_send.at[1],
+        recv_sem=swap_recv.at[1],
+        device_id=device(z, x, c, 1 - y),
+        device_id_type=MESH,
+    )
+    turn.start()
+    token_rows(2, 0, slice(0, half))
+    kept = pltpu.make_async_copy(acc.at[pl.ds(0, half)], gtok_o.at[y, 0], out_sem.at[0])
+    kept.start()
+    advance(18, TICKS)
+    turn.wait()
+    acc[half:rows, :] = home[...].astype(F32)
+    came = pltpu.make_async_copy(acc.at[pl.ds(half, half)], gtok_o.at[1 - y, 0], out_sem.at[1])
+    came.start()
+    away.wait()
+
+    def finish(index, carry):
+        scatter_sent(mode_of(c, index), gw.at[index], views(index), send.at[index], recv.at[index], pos)
+        return carry
+
+    lax.fori_loop(0, CHUNKS, finish, 0)
+    scatter_sent(mode_of(c, 0), small_g, small_bufs, send.at[CHUNKS], recv.at[CHUNKS], pos)
+    kept.wait()
+    came.wait()
+
+
+def backward_pass(wfa, wfd, saved, vec, rows_in, kaug):
+    rows, width = saved[0].shape
+    six = (4, 2, 2, 2)
+    vmem = pl.BlockSpec(memory_space=VMEM)
+    hbm = pl.BlockSpec(memory_space=ANY)
+    dma = pltpu.SemaphoreType.DMA
+
+    def buffers(rows, width, depth, count):
+        return [
+            VMEM(depth + (4, 2, 2, rows, width), BF16),
+            VMEM(count + (4, 2, rows, width), BF16),
+            VMEM(count + (6, rows, width), BF16),
+            VMEM(count + (3, rows, width), BF16),
+        ]
+
+    return pl.pallas_call(
+        backward_kernel,
+        out_shape=(
+            jax.ShapeDtypeStruct((CHUNKS,) + six + (32, width), BF16),
+            jax.ShapeDtypeStruct((2, 1, rows // 2, width), BF16),
+            jax.ShapeDtypeStruct((2, 1, rows // 2, width), F32),
+            jax.ShapeDtypeStruct((CHUNKS, 32, width), F32),
+            jax.ShapeDtypeStruct((16, 128), F32),
+        ),
+        in_specs=[hbm] * 15 + [vmem] * 3,
+        out_specs=[hbm] * 3 + [vmem] * 2,
+        scratch_shapes=[
+            VMEM((rows, width), F32),
+            VMEM((2, 128, width), F32),
+            VMEM((rows, width), BF16),
+            VMEM((rows, width), BF16),
+            VMEM((4, rows, width), BF16),
+            VMEM((2, rows, width), BF16),
+            VMEM((2,) + six + (32, width), BF16),
+            VMEM((2, 4, 2, 2, 2, 128, 256), BF16),
+            VMEM((2,) + six + (32, width), BF16),
+            VMEM((2, 4, 2, 2, 32, width), BF16),
+        ]
+        + buffers(32, width, (DEPTH,), (CHUNKS,))
+        + [
+            VMEM((rows // 2, width), BF16),
+            VMEM((8, width), F32),
+            VMEM((32, width), F32),
+            VMEM(six + (16, 128), BF16),
+            VMEM((4, 2, 2, 16, 128), BF16),
+        ]
+        + buffers(16, 128, (), ())
+        + [
+            dma((CHUNKS + 1, SLOTS)),
+            dma((CHUNKS + 1, SLOTS)),
+            dma((3,)),
+            pltpu.SemaphoreType.REGULAR,
+            dma((2,)),
+            dma((2,)),
+            dma((11,)),
+            dma((2,)),
+            dma((2,)),
+            dma((2,)),
+            dma((2,)),
+            dma((2,)),
+        ],
+        compiler_params=pltpu.CompilerParams(collective_id=1, has_side_effects=True, vmem_limit_bytes=62 * 1024 * 1024),
+        cost_estimate=pl.CostEstimate(flops=2 * 32 * rows * width * width, bytes_accessed=90 << 20, transcendentals=1 << 24),
+        name="backward_pass",
+    )(wfa, wfd, *saved, vec, rows_in, kaug)
+
+
+def paired(
+    tokens, lengths, w_query, w_key, w_value, w_out, w_up, w_down, vectors, up_bias, cotangent
+):
+    half, width = tokens.shape[2:]
+    rows = 2 * half
+    y = lax.axis_index("seq")
+    rank = lax.axis_index("dp") * 2 + y
+    spot = jnp.tile(vectors, (1, 4)) * (jnp.arange(128) // 32 == rank % 4).astype(BF16)
+    sm = jnp.concatenate([spot, up_bias[None, :], jnp.zeros((7, 128), BF16)])
+    length = lax.dynamic_index_in_dim(lengths[:, 0], y, keepdims=False)
+    near = jnp.arange(half, dtype=jnp.int32)
+    position = jnp.concatenate([y * half + near, (1 - y) * half + near])
+    ok = position < length
+    valid = jnp.broadcast_to(ok[:, None], (rows, 128)).astype(F32)
+    sixty = jnp.arange(128) % 64
+    bias = jnp.where(ok, 0.0, -1e9)[:, None]
+    kaug = jnp.where(sixty == 0, bias, ((sixty > 0) & (sixty < 4)).astype(F32)).astype(BF16)
+    weights = (w_query, w_key, w_value, w_out, w_up, w_down)
+    wfa, wfd, _, *saved, vec, rows_in = forward_pass(weights, sm, tokens, cotangent, kaug, valid)
+    _, activations, grad_tokens, outs, small = backward_pass(wfa, wfd, saved, vec, rows_in, kaug)
+    cut = width // 2
+    shard = outs.shape[1]
+    return (
+        activations,
+        grad_tokens,
+        jnp.concatenate([outs[9, :, :cut], outs[10, :, cut:]], axis=1),
+        jnp.concatenate([outs[9, :, cut:], outs[11, :, :cut]], axis=1),
+        jnp.concatenate([outs[10, :, :cut], outs[11, :, cut:]], axis=1),
+        outs[8],
+        outs[4:8].transpose(1, 0, 2).reshape(shard, 4 * width),
+        outs[0:4].reshape(4, shard, 4, width // 4).transpose(2, 1, 0, 3).reshape(4 * shard, width),
+        lax.dynamic_slice_in_dim(small[0:8], (rank % 4) * 32, 32, axis=1),
+        small[8],
+    )
+
+
 def solution(mesh):
     placed = (
         P(None, "dp", "seq", None),
@@ -267,8 +1326,9 @@
         P(("dp", "seq")),
         P(None, "dp", "seq", None),
     )
+    own = mesh.shape["dp"] == 16 and mesh.shape["seq"] == 2
     return jax.shard_map(
-        per_device,
+        paired if own else per_device,
         mesh=mesh,
         in_specs=placed,
         out_specs=(

time: 2270 us -> 468 us (0.21)
  waiting for transfers between devices: 1510 us -> 0 us
  Pallas kernels: 0 us -> 438 us
  matrix products: 414 us -> 0 us
  blocking collectives: 161 us -> 0 us
  other arithmetic: 108 us -> 4.91 us
  local copies, waits for them, and re-layouts: 53.1 us -> 16.7 us
    reduce_scatter x7 -> x0, waiting for transfers between devices: 825 us -> none  [the longest x1 361 us: per_device(): lax.psum_scatter(sums[4], ('dp', 'seq'), scatter_dimension=0, tiled=True)]
    pallas_call x0 -> x2, Pallas kernels: none -> 438 us  [the longest x1 223 us: backward_pass(): pl.pallas_call(backward_kernel, out_shape=(jax.ShapeDtypeStruct((CHUNKS,)...]
    unnamed x25 -> x0, waiting for transfers between devices: 428 us -> none
    dot_general x48 -> x0, matrix products: 414 us -> none  [the longest x2 46.5 us: per_device(): jnp.einsum('qhd,khd->hqk', grad_ctx_heads, val_heads, preferred_element_t...]
    all_gather x10 -> x0, waiting for transfers between devices: 252 us -> none  [the longest x1 67.1 us: fetch_forward(): lax.all_gather(w_down, ('dp', 'seq'), axis=0, tiled=True)]
    all_gather x2 -> x0, blocking collectives: 122 us -> none  [the longest x1 61.5 us: fetch_forward(): lax.all_gather(vectors, ('dp', 'seq'), axis=1, tiled=True)]
    convert_element_type x4 -> x3, other arithmetic: 59.2 us -> 1.57 us  [the longest x1 0.91 us: paired(): jnp.where(sixty == 0, bias, ((sixty > 0) & (sixty < 4)).astype(F32))]
    reduce_sum x11 -> x0, other arithmetic: 43.6 us -> none  [the longest x2 29.4 us: per_device(): jnp.sum(jnp.exp(scores - top), axis=-1, keepdims=True)]
  transfers between devices with their start and end apart: 21 -> 0, of which waited for: 14 -> 0; matrix products, arithmetic and copies ran while one was open for 20% -> 0% of each run, Pallas kernels for 0% -> 0%
where the time goes in v2:
time: 468 us; the launch traced here: 461 us
  Pallas kernels  438 us (94%)
  local copies, waits for them, and re-layouts  16.7 us (4%)
  other arithmetic  4.91 us (1%)
    pallas_call x1, Pallas kernels, backward_pass(): pl.pallas_call(backward_kernel, out_shape=(jax.ShapeDtypeStruct((CHUNKS,)...  223 us
    pallas_call x1, Pallas kernels, forward_pass(): pl.pallas_call(forward_kernel, out_shape=(jax.ShapeDtypeStruct((8,) + six...  215 us

profile of v2, /device:TPU:5, one launch (start us, length us, event | category | flops | bytes accessed | tf_op | source)
XLA Modules:
  0.0 461.1 jit_solution(968243686450645072)
XLA Ops:
  0.6 0.0 copy-start
  0.7 0.6 copy-done
  1.3 0.6 constant_dynamic-slice_fusion.1
  1.9 0.1 pad.10.clone
  2.0 0.7 fusion
  2.7 0.7 tile.4
  3.4 0.1 tile.10
  3.5 1.3 maximum_maximum_fusion.sm
  4.8 0.9 select_convert_fusion.kaug
  5.7 1.0 broadcast_in_dim.45.valid
  6.7 214.9 %forward_pass.1 = (bf16[8,4,2,2,2,32,1024]{6,5,4,3,2,1,0:T(8,128)(2,1)}, bf16[4,4,2,2,2,128,256]{6,5,4,3,2,1,0:T(8,128)(2,1)}, bf16[4,2,2,2,16,128]{5,4,3,2,1,0:...) custom-call(bf16[32,1024]{1,0:T(8,128)(2,1)} %wq.1, ...), custom_call_target="tpu_custom_call" | custom-call | flops 30064771072 | bytes 94371840 | tf_op jit(solution)/shard_map/forward_pass/pallas_call | solution.py:701
  221.6 223.4 %backward_pass.1 = (bf16[12,4,2,2,2,32,1024]{6,5,4,3,2,1,0:T(8,128)(2,1)}, bf16[2,1,512,1024]{3,2,1,0:T(8,128)(2,1)}, f32[2,1,512,1024]{3,2,1,0:T(8,128)}, f32[12,32,1024]{2,1,0:T(8,128)}, f32[16,128]{1,0:T(8,128)}) custom-call(bf16[8,4,2,2,2,32,1024]{6,5,4,3,2,1,0:T(8,128)(2,1)} %get-tuple-element.31.wfa, ...), custom_call_target="tpu_custom_call" | custom-call | flops 68719476736 | bytes 94371840 | tf_op jit(solution)/shard_map/backward_pass/pallas_call | solution.py:1227
  445.0 1.2 slice_bitcast_fusion.8
  446.1 0.7 slice.42
  446.8 0.7 constant_dynamic-slice_fusion
  447.5 1.6 slice_bitcast_fusion.1
  449.1 1.0 slice_bitcast_fusion.3
  450.1 1.3 fusion.1
  451.4 0.2 reshape.73
  451.6 0.0 copy-start.3
  451.6 0.3 copy.23
  452.0 0.9 copy.25
  452.9 0.7 pad_maximum_fusion.2
  453.5 0.7 pad_maximum_fusion.1
  454.2 0.7 pad_maximum_fusion
  454.9 0.8 copy.24
  455.7 0.0 copy-done.3
  455.7 0.0 copy-start.2
  455.7 1.3 copy.28
  457.0 1.6 copy-done.2
  458.6 0.0 copy-start.1
  458.6 2.0 copy.29
  460.7 0.0 copy-done.1
  (6 shorter events, 0.0 us)
Async XLA Ops:
  0.6 0.7 copy-start
  451.6 4.1 copy-start.3
  455.7 2.9 copy-start.2
  458.6 2.0 copy-start.1
